TPU v7x, 128 devices: a whole 4x4x4 slice. The times are simulated.
128 devices in a mesh: ctx: 64 (over y_hi, x, z, core), mp: 2 (over y_lo).
Axes of the slice: x: 4, y: 4 (y_hi: 2, y_lo: 2; y = y_hi * 2 + y_lo), z: 4, core: 2. Of those that a mesh axis runs over, the one named last changes fastest.
Arguments:
- tokens: bfloat16 [8192, 768], P('ctx'), may hold values from -6 to 6
- attn_gain: float32 [768], replicated, may hold values from 0.5 to 1.5
- w_query: bfloat16 [768, 768], P(None, 'mp'), may hold values from -0.0546875 to 0.0546875
- w_key: bfloat16 [768, 768], P(None, 'mp'), may hold values from -0.21875 to 0.21875
- w_value: bfloat16 [768, 768], P(None, 'mp'), may hold values from -0.21875 to 0.21875
- w_proj: bfloat16 [768, 768], P('mp'), may hold values from -2 to 2
- rel_table: float32 [32, 12], P(None, 'mp'), may hold values from -6 to 6
- rel_bucket: int32 [16383], replicated, may hold values from 0 to 31, as said below
- ffn_gain: float32 [768], replicated, may hold values from 0.5 to 1.5
- router: float32 [768, 64], replicated, may hold values from -0.15625 to 0.15625
- w_in: bfloat16 [64, 768, 3072], P('ctx', None, 'mp'), may hold values from -0.21875 to 0.21875
- w_out: bfloat16 [64, 3072, 768], P('ctx', 'mp'), may hold values from -10 to 10
- expert_route: int32 [8192], P('ctx'), may hold values from 0 to 63, as said below
- expert_slot: int32 [8192], P('ctx'), may hold values from 0 to 3, as said below
- cotangent: bfloat16 [8192, 768], P('ctx'), may hold values from -6 to 6
Outputs:
- mixed: bfloat16 [8192, 768], P('ctx')
- grad_input: float32 [8192, 768], P('ctx')
- grad_attn_gain: float32 [768], replicated
- grad_query: float32 [768, 768], P(None, 'mp')
- grad_key: float32 [768, 768], P(None, 'mp')
- grad_value: float32 [768, 768], P(None, 'mp')
- grad_proj: float32 [768, 768], P('mp')
- grad_table: float32 [32, 12], P(None, 'mp')
- grad_ffn_gain: float32 [768], replicated
- grad_router: float32 [768, 64], replicated
- grad_expert_in: float32 [64, 768, 3072], P('ctx', None, 'mp')
- grad_expert_out: float32 [64, 3072, 768], P('ctx', 'mp')
Inputs may be any that keep to these rules, and one draw needn't show every extreme that they name: `rel_bucket`: entry 8191 + r is the bucket of the offset r = key position - query position: offsets of size under 8 have buckets 0 to 7, larger sizes share buckets 8 to 15 that never fall as the size grows, and positive offsets add 16. `expert_route`: of the 128 tokens of one device, at most 4 go to one expert, and one expert gets exactly 4 tokens from every device. `expert_slot`: tokens of one device with the same expert have distinct slots.
All inputs are finite; a program needn't handle non-finite values.
Results may differ from a plain program's by a relative error of at most 0.024.
Values may be sent and summed in bfloat16 or wider, within the bound.
A program may use at most 192 MiB of HBM per device.

v0:
```python
import functools
import jax
import jax.numpy as jnp
from jax import lax
from jax.experimental import pallas as pl
from jax.experimental.pallas import tpu as pltpu
from jax.sharding import PartitionSpec as P

HEAD = 64
GROUP = 3
BLOCK = 128
PAIR = 2 * BLOCK
FORWARD_SPAN = 8
BACKWARD_SPAN = 4
VMEM = pl.BlockSpec(memory_space=pltpu.VMEM)
SMEM = pl.BlockSpec(memory_space=pltpu.SMEM)
LARGE = pltpu.CompilerParams(vmem_limit_bytes=60 * 1024 * 1024)


def contract(left, right, left_dim, right_dim):
    return lax.dot_general(
        left,
        right,
        (((left_dim,), (right_dim,)), ((), ())),
        preferred_element_type=jnp.float32,
    )


def window_row(place, chunk, tile, half, span):
    return 63 - (span * chunk + tile // 2) + place + BLOCK // 4 * (half - tile % 2)


def tile_consts(table_ref, head, place, chunk, tile, span):
    parts = []
    for half in range(2):
        row = window_row(place, chunk, tile, half, span)
        parts.append(jnp.broadcast_to(table_ref[head, pl.ds(row, 1), 0:1], (1, BLOCK)))
    return jnp.concatenate(parts, axis=1)


def chunk_mixed(uneven_ref, place, chunk, span):
    mixed = 0
    for tile in range(2 * span):
        for half in range(2):
            mixed = mixed + uneven_ref[0, window_row(place, chunk, tile, half, span)]
    return mixed


def add_uneven(table_ref, uneven_ref, score_ref, place, chunk, span):
    for tile in range(2 * span):
        for half in range(2):
            row = window_row(place, chunk, tile, half, span)

            @pl.when(uneven_ref[0, row] > 0)
            def _():
                for head in range(GROUP):
                    window = jnp.concatenate(
                        [table_ref[head, pl.ds(row, 1), :], table_ref[head, pl.ds(row + 1, 1), :]],
                        axis=1,
                    )
                    window = window - window[:, 0:1]
                    grid = pltpu.roll(
                        jnp.broadcast_to(window, (BLOCK, PAIR)),
                        BLOCK,
                        1,
                        stride=1,
                        stride_axis=0,
                    )[:, :BLOCK]
                    rows = slice(tile * BLOCK, (tile + 1) * BLOCK)
                    cols = slice(half * BLOCK, (half + 1) * BLOCK)
                    score_ref[head, rows, cols] += grid


def stream(keys_hbm, held_ref, sems, span):
    def copy(chunk):
        slot = lax.rem(chunk, 2)
        return pltpu.make_async_copy(
            keys_hbm.at[pl.ds(chunk * span, span)], held_ref.at[slot], sems.at[slot]
        )

    return copy


def head_columns(ref, head):
    return ref[:, head * HEAD : (head + 1) * HEAD]


def turn(values):
    return values.astype(jnp.float32).T


def fill_turned(dst_ref, src_ref, first):
    for head in range(GROUP):
        part = turn(head_columns(src_ref, head))
        none = jnp.zeros_like(part)
        parts = [part, none] if first else [none, part]
        dst_ref[head] = jnp.concatenate(parts, axis=0).astype(dst_ref.dtype)


def fill_padded(dst_ref, src_ref, first):
    for head in range(GROUP):
        part = head_columns(src_ref, head)
        none = jnp.zeros_like(part)
        parts = [part, none] if first else [none, part]
        dst_ref[head] = jnp.concatenate(parts, axis=1)


def side_by_side(parts):
    return jnp.concatenate([turn(part) for part in parts], axis=1).astype(jnp.bfloat16)


def flip_both(values):
    down = lax.broadcasted_iota(jnp.int32, (BLOCK, BLOCK), 0)
    right = lax.broadcasted_iota(jnp.int32, (BLOCK, BLOCK), 1)
    anti = jnp.where(down + right == BLOCK - 1, 1.0, 0.0).astype(jnp.bfloat16)
    once = contract(anti, values.astype(jnp.float32).astype(jnp.bfloat16), 1, 0)
    return contract(once.astype(jnp.bfloat16), anti, 1, 0).astype(jnp.int32)


def line_of(column):
    down = lax.broadcasted_iota(jnp.int32, (BLOCK, BLOCK), 0)
    right = lax.broadcasted_iota(jnp.int32, (BLOCK, BLOCK), 1)
    return jnp.sum(jnp.where(down == right, column, 0.0), axis=0, keepdims=True)


def shifted_up(column):
    return jnp.concatenate([column[1:], column[-1:]], axis=0)


def forward_kernel(
    place_ref, rel_ref, buckets_ref, keys_hbm, rows_ref,
    out_ref, turned_ref, lse_ref, flipped_ref, table_ref, uneven_out_ref,
    held_ref, held_sem, uneven_ref, uneven_sem,
    query_ref, best_ref, sum_ref, total_ref, score_ref,
):
    place = place_ref[0]
    span = FORWARD_SPAN
    tiles, length = 2 * span, PAIR * span
    fetch = stream(keys_hbm, held_ref, held_sem, span)
    chunks = keys_hbm.shape[0] // span
    fetch(0).start()
    flipped = flip_both(buckets_ref[...])
    flipped_ref[...] = flipped
    floats = flipped.astype(jnp.float32)
    high = jnp.max(floats, axis=1, keepdims=True)
    low = jnp.min(floats, axis=1, keepdims=True)
    high = jnp.maximum(high, shifted_up(high))
    low = jnp.minimum(low, shifted_up(low))
    uneven_out_ref[...] = line_of(jnp.where(high > low, 1.0, 0.0)).astype(jnp.int32)
    flags = pltpu.make_async_copy(uneven_out_ref, uneven_ref, uneven_sem)
    flags.start()
    for head in range(GROUP):
        values = jnp.zeros((BLOCK, BLOCK), jnp.float32)
        for bucket in range(rel_ref.shape[0]):
            value = rel_ref[bucket, place_ref[1] * GROUP + head]
            values = jnp.where(flipped == bucket, value, values)
        table_ref[head] = values
    fill_turned(query_ref, rows_ref, True)
    flags.wait()
    best_ref[...] = jnp.full_like(best_ref, -1e30)
    sum_ref[...] = jnp.zeros_like(sum_ref)
    total_ref[...] = jnp.zeros_like(total_ref)

    def rest(chunk, head, held, scores):
        consts = [tile_consts(table_ref, head, place, chunk, tile, span) for tile in range(tiles)]
        old = best_ref[head]
        new = old
        for tile in range(tiles):
            part = scores[tile * BLOCK : (tile + 1) * BLOCK]
            new = jnp.maximum(new, jnp.max(part, axis=0, keepdims=True) + consts[tile])
        decay = jnp.exp(old - new)
        weights = [
            jnp.exp(scores[tile * BLOCK : (tile + 1) * BLOCK] - (new - consts[tile]))
            for tile in range(tiles)
        ]
        weights = jnp.concatenate(weights, axis=0)
        sum_ref[head] = sum_ref[head] * decay + jnp.sum(weights, axis=0, keepdims=True)
        best_ref[head] = new
        total_ref[head] = total_ref[head] * decay + contract(
            held, weights.astype(jnp.bfloat16), 0, 0
        )

    @pl.loop(0, chunks)
    def _(chunk):
        slot = lax.rem(chunk, 2)
        fetch(chunk).wait()

        @pl.when(chunk + 1 < chunks)
        def _():
            fetch(chunk + 1).start()

        def held_of(head):
            return held_ref[slot, :, head].reshape(length, 2 * HEAD)

        mixed = chunk_mixed(uneven_ref, place, chunk, span)

        @pl.when(mixed == 0)
        def _():
            helds = [held_of(head) for head in range(GROUP)]
            scores = [contract(helds[head], query_ref[head], 1, 0) for head in range(GROUP)]
            for head in range(GROUP):
                rest(chunk, head, helds[head], scores[head])

        @pl.when(mixed > 0)
        def _():
            for head in range(GROUP):
                score_ref[head] = contract(held_of(head), query_ref[head], 1, 0)
            add_uneven(table_ref, uneven_ref, score_ref, place, chunk, span)
            for head in range(GROUP):
                rest(chunk, head, held_of(head), score_ref[head])

    for head in range(GROUP):
        turned_ref[head] = total_ref[head][HEAD:] / sum_ref[head]
    out_ref[...] = side_by_side([turned_ref[head] for head in range(GROUP)])
    for head in range(GROUP):
        lse_ref[head] = best_ref[head] + jnp.log(sum_ref[head])


def backward_kernel(
    place_ref, uneven_ref, table_ref, keys_hbm, rows_ref, grads_ref, turned_ref, lse_ref,
    flipped_ref, rows_in_ref, rows_grad_ref, activ_ref, grad_pre_ref,
    grad_keys_hbm, grad_rows_ref, slab_ref, expert_in_hbm, expert_out_hbm,
    held_ref, held_sem, grad_keys_ref, grad_keys_sem, expert_in, expert_out, expert_sem, offsets_ref, query_t_ref, grad_t_ref, query_ref, grad_ref, delta_ref, grad_query_ref, score_ref,
):
    place = place_ref[0]
    span = BACKWARD_SPAN
    tiles, length = 2 * span, PAIR * span
    fetch = stream(keys_hbm, held_ref, held_sem, span)
    chunks = keys_hbm.shape[0] // span
    fetch(0).start()

    def give(chunk):
        slot = lax.rem(chunk, 2)
        return pltpu.make_async_copy(
            grad_keys_ref.at[slot],
            grad_keys_hbm.at[pl.ds(chunk * span, span)],
            grad_keys_sem.at[slot],
        )

    expert_in[...] = contract(rows_in_ref[...], grad_pre_ref[...], 0, 0)
    expert_out[...] = contract(activ_ref[...], rows_grad_ref[...], 0, 0)
    stores = [
        pltpu.make_async_copy(expert_in, expert_in_hbm, expert_sem.at[0]),
        pltpu.make_async_copy(expert_out, expert_out_hbm, expert_sem.at[1]),
    ]
    for store in stores:
        store.start()
    fill_turned(query_t_ref, rows_ref, True)
    fill_turned(grad_t_ref, grads_ref, False)
    fill_padded(query_ref, rows_ref, True)
    fill_padded(grad_ref, grads_ref, False)
    for head in range(GROUP):
        delta_ref[head] = jnp.sum(
            grad_t_ref[head][HEAD:].astype(jnp.float32) * turned_ref[head], axis=0, keepdims=True
        )
    grad_query_ref[...] = jnp.zeros_like(grad_query_ref)
    offsets_ref[...] = jnp.zeros_like(offsets_ref)

    def rest(chunk, head, held, scores, grads):
        probs = jnp.concatenate(
            [
                jnp.exp(
                    scores[tile * BLOCK : (tile + 1) * BLOCK]
                    - (lse_ref[head] - tile_consts(table_ref, head, place, chunk, tile, span))
                )
                for tile in range(tiles)
            ],
            axis=0,
        )
        slopes = probs * (grads - delta_ref[head])
        rounded = slopes.astype(jnp.bfloat16)
        part = contract(rounded, query_ref[head], 1, 0) + contract(
            probs.astype(jnp.bfloat16), grad_ref[head], 1, 0
        )
        grad_keys_ref[lax.rem(chunk, 2), :, head] = part.astype(grad_keys_ref.dtype).reshape(
            span, PAIR, 2 * HEAD
        )
        grad_query_ref[head] += contract(held, rounded, 0, 0)
        return slopes

    def put_even(chunk, head, tile, half, slopes):
        row = window_row(place, chunk, tile, half, span)
        offsets_ref[head, pl.ds(row, 1), :] += jnp.sum(slopes, axis=0, keepdims=True)

    def put_uneven(chunk, head, tile, half, slopes):
        row = window_row(place, chunk, tile, half, span)
        wide = jnp.concatenate([slopes, jnp.zeros_like(slopes)], axis=1)
        folded = jnp.zeros((8, PAIR), jnp.float32)
        for group in range(BLOCK // 8):
            folded = folded + pltpu.roll(
                wide[group * 8 : (group + 1) * 8], (BLOCK - 8 * group) % PAIR, 1
            )
        line = jnp.zeros((1, PAIR), jnp.float32)
        for step in range(8):
            line = line + pltpu.roll(folded, (PAIR - step) % PAIR, 1)[step : step + 1]
        offsets_ref[head, pl.ds(row, 1), :] += line[:, :BLOCK]
        offsets_ref[head, pl.ds(row + 1, 1), :] += line[:, BLOCK:]

    @pl.loop(0, chunks)
    def _(chunk):
        slot = lax.rem(chunk, 2)
        fetch(chunk).wait()

        @pl.when(chunk + 1 < chunks)
        def _():
            fetch(chunk + 1).start()

        def held_of(head):
            return held_ref[slot, :, head].reshape(length, 2 * HEAD)

        @pl.when(chunk >= 2)
        def _():
            give(chunk - 2).wait()

        mixed = chunk_mixed(uneven_ref, place, chunk, span)

        @pl.when(mixed == 0)
        def _():
            helds = [held_of(head) for head in range(GROUP)]
            scores = [contract(helds[head], query_t_ref[head], 1, 0) for head in range(GROUP)]
            grads = [contract(helds[head], grad_t_ref[head], 1, 0) for head in range(GROUP)]
            for head in range(GROUP):
                slopes = rest(chunk, head, helds[head], scores[head], grads[head])
                for tile in range(tiles):
                    for half in range(2):
                        part = slopes[
                            tile * BLOCK : (tile + 1) * BLOCK, half * BLOCK : (half + 1) * BLOCK
                        ]
                        put_even(chunk, head, tile, half, part)

        @pl.when(mixed > 0)
        def _():
            for head in range(GROUP):
                score_ref[head] = contract(held_of(head), query_t_ref[head], 1, 0)
            add_uneven(table_ref, uneven_ref, score_ref, place, chunk, span)
            for head in range(GROUP):
                held = held_of(head)
                grads = contract(held, grad_t_ref[head], 1, 0)
                score_ref[head] = rest(chunk, head, held, score_ref[head], grads)
            for tile in range(tiles):
                for half in range(2):
                    rows = slice(tile * BLOCK, (tile + 1) * BLOCK)
                    cols = slice(half * BLOCK, (half + 1) * BLOCK)
                    uneven = uneven_ref[0, window_row(place, chunk, tile, half, span)]

                    @pl.when(uneven == 0)
                    def _():
                        for head in range(GROUP):
                            put_even(chunk, head, tile, half, score_ref[head, rows, cols])

                    @pl.when(uneven > 0)
                    def _():
                        for head in range(GROUP):
                            put_uneven(chunk, head, tile, half, score_ref[head, rows, cols])

        give(chunk).start()

    for chunk in (chunks - 2, chunks - 1):
        give(chunk).wait()
    grad_rows_ref[...] = side_by_side([grad_query_ref[head][:HEAD] for head in range(GROUP)])
    lanes = lax.broadcasted_iota(jnp.int32, (1, BLOCK), 1)
    for bucket in range(slab_ref.shape[0]):
        hit = flipped_ref[...] == bucket
        line = jnp.zeros((1, BLOCK), jnp.float32)
        for head in range(GROUP):
            part = jnp.sum(jnp.where(hit, offsets_ref[head], 0.0), axis=0, keepdims=True)
            part = jnp.sum(part, axis=1, keepdims=True)
            line = jnp.where(lanes == place_ref[1] * GROUP + head, part, line)
        slab_ref[pl.ds(bucket, 1)] = line
    for store in stores:
        store.wait()


def attend(place, rel_table, buckets, keys, rows):
    shape = jax.ShapeDtypeStruct
    anywhere = pl.BlockSpec(memory_space=pl.ANY)
    return pl.pallas_call(
        forward_kernel,
        out_shape=(
            shape(rows.shape, jnp.bfloat16),
            shape((GROUP, HEAD, PAIR), jnp.float32),
            shape((GROUP, 1, PAIR), jnp.float32),
            shape((BLOCK, BLOCK), jnp.int32),
            shape((GROUP, BLOCK, BLOCK), jnp.float32),
            shape((1, BLOCK), jnp.int32),
        ),
        in_specs=[SMEM, SMEM, VMEM, anywhere, VMEM],
        out_specs=(VMEM,) * 6,
        scratch_shapes=[
            pltpu.VMEM((2, FORWARD_SPAN) + keys.shape[1:], keys.dtype),
            pltpu.SemaphoreType.DMA((2,)),
            pltpu.SMEM((1, BLOCK), jnp.int32),
            pltpu.SemaphoreType.DMA,
            pltpu.VMEM((GROUP, 2 * HEAD, PAIR), jnp.bfloat16),
            pltpu.VMEM((GROUP, 1, PAIR), jnp.float32),
            pltpu.VMEM((GROUP, 1, PAIR), jnp.float32),
            pltpu.VMEM((GROUP, 2 * HEAD, PAIR), jnp.float32),
            pltpu.VMEM((GROUP, FORWARD_SPAN * PAIR, PAIR), jnp.float32),
        ],
        compiler_params=LARGE,
        name="attend",
    )(place, rel_table, buckets, keys, rows)


def attend_back(
    place, uneven, table, keys, rows, grads, turned, lse, flipped, rows_in, rows_grad, activ,
    grad_pre, buckets,
):
    shape = jax.ShapeDtypeStruct
    wide_row, hidden = rows_in.shape[1], activ.shape[1]
    anywhere = pl.BlockSpec(memory_space=pl.ANY)
    return pl.pallas_call(
        backward_kernel,
        out_shape=(
            shape(keys.shape, jnp.bfloat16),
            shape(rows.shape, jnp.bfloat16),
            shape((buckets, BLOCK), jnp.float32),
            shape((wide_row, hidden), jnp.float32),
            shape((hidden, wide_row), jnp.float32),
        ),
        in_specs=[SMEM, SMEM, VMEM, anywhere] + [VMEM] * 9,
        out_specs=(anywhere, VMEM, VMEM, anywhere, anywhere),
        scratch_shapes=[
            pltpu.VMEM((2, BACKWARD_SPAN) + keys.shape[1:], keys.dtype),
            pltpu.SemaphoreType.DMA((2,)),
            pltpu.VMEM((2, BACKWARD_SPAN) + keys.shape[1:], keys.dtype),
            pltpu.SemaphoreType.DMA((2,)),
            pltpu.VMEM((wide_row, hidden), jnp.float32),
            pltpu.VMEM((hidden, wide_row), jnp.float32),
            pltpu.SemaphoreType.DMA((2,)),
            pltpu.VMEM((GROUP, BLOCK, BLOCK), jnp.float32),
            pltpu.VMEM((GROUP, 2 * HEAD, PAIR), jnp.bfloat16),
            pltpu.VMEM((GROUP, 2 * HEAD, PAIR), jnp.bfloat16),
            pltpu.VMEM((GROUP, PAIR, 2 * HEAD), jnp.bfloat16),
            pltpu.VMEM((GROUP, PAIR, 2 * HEAD), jnp.bfloat16),
            pltpu.VMEM((GROUP, 1, PAIR), jnp.float32),
            pltpu.VMEM((GROUP, 2 * HEAD, PAIR), jnp.float32),
            pltpu.VMEM((GROUP, BACKWARD_SPAN * PAIR, PAIR), jnp.float32),
        ],
        compiler_params=LARGE,
        name="attend_back",
    )(
        place, uneven, table, keys, rows, grads, turned, lse, flipped, rows_in, rows_grad, activ,
        grad_pre,
    )


EPSILON = 1e-06
PRECISE = lax.Precision.HIGHEST
ANYWHERE = pl.BlockSpec(memory_space=pl.ANY)
SIDE = 4


class Place:
    def __init__(self):
        self.me = lax.axis_index("ctx")
        self.core = lax.rem(self.me, 2)
        self.z = lax.rem(self.me // 2, SIDE)
        self.x = lax.rem(self.me // (2 * SIDE), SIDE)
        self.y = self.me // (2 * SIDE * SIDE)

    def at(self, dx=0, dz=0, dcore=0, dy=0):
        x = lax.rem(self.x + dx, SIDE)
        z = lax.rem(self.z + dz, SIDE)
        core = lax.rem(self.core + dcore, 2)
        y = lax.rem(self.y + dy, 2)
        return ((y * SIDE + x) * SIDE + z) * 2 + core

    def turned(self, axis, step):
        return self.at(dx=step) if axis == 0 else self.at(dz=step)

    def along(self, axis, step):
        return lax.rem((self.x if axis == 0 else self.z) + step, SIDE)


def greet(targets, across=False):
    barrier = pltpu.get_barrier_semaphore()
    if across:
        pl.semaphore_signal(
            barrier,
            inc=1,
            device_id={"mp": 1 - lax.axis_index("mp")},
            device_id_type=pl.DeviceIdType.MESH,
        )
    for target in targets:
        pl.semaphore_signal(
            barrier, inc=1, device_id={"ctx": target}, device_id_type=pl.DeviceIdType.MESH
        )
    return barrier, len(targets) + int(across)


def meet(targets, across=False):
    pl.semaphore_wait(*greet(targets, across))


def ring_targets(place):
    found = [place.at(dcore=1)]
    for step in range(1, SIDE):
        found += [place.at(dx=step), place.at(dz=step)]
    return found


def sender(target, src, dst, send_sem, recv_sem):
    return pltpu.make_async_remote_copy(
        src_ref=src,
        dst_ref=dst,
        send_sem=send_sem,
        recv_sem=recv_sem,
        device_id={"ctx": target},
        device_id_type=pl.DeviceIdType.MESH,
    )


def wide(value):
    return value.astype(jnp.float32)


class Sends:
    def __init__(self, place, sems):
        self.place, self.sems, self.started = place, sems, []

    def go(self, target, src, dst, recv_sem):
        copy = sender(target, src, dst, self.sems.at[len(self.started)], recv_sem)
        copy.start()
        self.started.append(copy)
        return copy

    def across(self, src, dst, recv_sem):
        copy = pltpu.make_async_remote_copy(
            src_ref=src,
            dst_ref=dst,
            send_sem=self.sems.at[len(self.started)],
            recv_sem=recv_sem,
            device_id={"mp": 1 - lax.axis_index("mp")},
            device_id_type=pl.DeviceIdType.MESH,
        )
        copy.start()
        self.started.append(copy)

    def landed(self, view, sem):
        sender(self.place.me, view, view, sem, sem).wait_recv()

    def finish(self):
        for copy in self.started:
            copy.wait_send()


def gather_kernel(
    tokens_ref, gain_ref, w_query_ref, w_key_ref, w_value_ref,
    normed_ref, rows_ref, out_ref,
    block_ref, given, other, local_sem, send_sem, ring_recv, twin_recv, swap_recv,
):
    place = Place()
    barrier = greet(ring_targets(place) + [place.at(dy=1)])
    sends = Sends(place, send_sem)
    half_rows = block_ref.shape[1] // 2
    sub_rows = half_rows // 2
    first = place.y == 0
    width = GROUP * HEAD
    floats_in = wide(tokens_ref[...])
    scale = lax.rsqrt(jnp.mean(floats_in * floats_in, axis=1, keepdims=True) + EPSILON)
    normed = (floats_in * scale * gain_ref[...][None]).astype(normed_ref.dtype)
    normed_ref[...] = normed
    kept = []
    for n, ref in enumerate((w_query_ref, w_key_ref, w_value_ref)):
        made = contract(normed, ref[...], 1, 0).astype(given.dtype)
        kept.append(jnp.where(first, made[:, :width], made[:, width:]))
        given[n] = jnp.where(first, made[:, width:], made[:, :width])

    def rows_at(half, start=0, count=half_rows):
        side = place.y if half == 0 else 1 - place.y
        return pl.ds(pl.multiple_of(side * half_rows + start, sub_rows), count)

    def put(half, query, key, value):
        rows_ref[rows_at(half)] = query
        for head in range(GROUP):
            lanes = slice(head * HEAD, (head + 1) * HEAD)
            block_ref[head, rows_at(half)] = jnp.concatenate(
                [key[:, lanes], value[:, lanes]], axis=1
            )

    put(0, *kept)
    pl.semaphore_wait(*barrier)
    sends.go(place.at(dy=1), given, other, swap_recv)

    def rows_of(half, piece):
        if piece is None:
            return rows_at(half)
        return rows_at(half, piece * sub_rows, sub_rows)

    def view(half, first, second, core, piece=None):
        x, z = (second, first) if half == 0 else (first, second)
        slot = (place.along(0, x) * SIDE + place.along(1, z)) * 2 + core
        return out_ref.at[slot, :, rows_of(half, piece)]

    def held(half, first, second, piece=None):
        if first == 0 and second == 0:
            return block_ref.at[:, rows_of(half, piece)]
        return view(half, first, second, place.core, piece)

    def shift(half, first, second, stage, step, piece=None):
        axis = 1 - half if stage == 0 else half
        if stage == 0:
            slot = ((first - step) % SIDE, second)
        else:
            slot = (first, (second - step) % SIDE)
        sends.go(
            place.turned(axis, step % SIDE),
            held(half, first, second, piece),
            view(half, first, second, place.core, piece),
            ring_recv.at[half, slot[0], slot[1], piece or 0],
        )

    def to_twin(half, first, second):
        sends.go(
            place.at(dcore=1),
            held(half, first, second),
            view(half, first, second, place.core),
            twin_recv.at[half, first, second],
        )

    def wait(half, first, second):
        if second == 2:
            for piece in range(2):
                sends.landed(
                    view(half, first, second, place.core, piece),
                    ring_recv.at[half, first, second, piece],
                )
        else:
            sends.landed(
                view(half, first, second, place.core), ring_recv.at[half, first, second, 0]
            )

    def relay(half, first, second):
        if second == SIDE - 1:
            shift(half, first, second, 1, 1, 0)
        elif second == 1:
            shift(half, first, second, 1, -1, 1)

    for half in range(2):
        if half == 1:
            sends.landed(other, swap_recv)
            put(1, other[0], other[1], other[2])
        for stage in range(2):
            for step in (1, -1, 2)[: 3 - stage]:
                shift(half, 0, 0, stage, step)
        to_twin(half, 0, 0)
    own = pltpu.make_async_copy(
        block_ref, out_ref.at[(place.x * SIDE + place.z) * 2 + place.core], local_sem
    )
    own.start()
    order = [(3, 0), (1, 0), (0, 3), (0, 1), (2, 0), (3, 3), (3, 1), (1, 3), (1, 1), (0, 2)]
    order += [(3, 2), (1, 2), (2, 3), (2, 1), (2, 2)]
    for first, second in order:
        for half in range(2):
            wait(half, first, second)
            if second == 0:
                for step in (1, -1):
                    shift(half, first, second, 1, step)
            else:
                relay(half, first, second)
            to_twin(half, first, second)
    for first, second in [(0, 0)] + order:
        for half in range(2):
            sends.landed(
                view(half, first, second, 1 - place.core), twin_recv.at[half, first, second]
            )
    own.wait()
    sends.finish()


def gather_plane(tokens, gain, w_query, w_key, w_value):
    kind = tokens.dtype
    tok_rows = tokens.shape[0]
    width = GROUP * HEAD
    block = (GROUP, 2 * tok_rows, 2 * HEAD)
    shape = jax.ShapeDtypeStruct
    sem = pltpu.SemaphoreType.DMA
    return pl.pallas_call(
        gather_kernel,
        out_shape=(
            shape(tokens.shape, kind),
            shape((2 * tok_rows, width), kind),
            shape((2 * SIDE * SIDE,) + block, kind),
        ),
        in_specs=[VMEM] * 5,
        out_specs=(VMEM, VMEM, ANYWHERE),
        scratch_shapes=[
            pltpu.VMEM(block, kind),
            pltpu.VMEM((3, tok_rows, width), kind),
            pltpu.VMEM((3, tok_rows, width), kind),
            sem, sem((73,)), sem((2, SIDE, SIDE, 2)), sem((2, SIDE, SIDE)), sem,
        ],
        compiler_params=pltpu.CompilerParams(
            collective_id=1, has_side_effects=True, vmem_limit_bytes=60 * 1024 * 1024
        ),
        name="gather_plane",
    )(tokens, gain, w_query, w_key, w_value)


def ring_sum(sends, axis_of, sums, via, landing, via_recv, land_recv, ready):
    place = sends.place
    rows = sums.shape[-2] // 2
    middle = (slice(None),) * (len(sums.shape) - 4)

    def cut(ref, index, piece):
        return ref.at[index + middle + (pl.ds(piece * rows, rows),)]

    for half in range(2):
        ready(half, 2)
        for piece, step in ((0, 1), (1, SIDE - 1)):
            sends.go(
                place.turned(axis_of(half), step),
                cut(sums, (half, 2), piece),
                via.at[half, piece],
                via_recv.at[half, piece],
            )
    for half in range(2):
        for piece, step in ((0, 1), (1, SIDE - 1)):
            ready(half, step)
            sends.go(
                place.turned(axis_of(half), step),
                cut(sums, (half, step), 1 - piece),
                cut(landing, (half, piece), 1 - piece),
                land_recv.at[half, piece, 1 - piece],
            )
    for half in range(2):
        ready(half, 0)
    for half in range(2):
        for piece, step in ((0, 1), (1, SIDE - 1)):
            sends.landed(via.at[half, piece], via_recv.at[half, piece])
            spot = (half, step) + middle + (slice(piece * rows, (piece + 1) * rows),)
            sums[spot] = (wide(sums[spot]) + wide(via[half, piece])).astype(sums.dtype)
            sends.go(
                place.turned(axis_of(half), step),
                cut(sums, (half, step), piece),
                cut(landing, (half, piece), piece),
                land_recv.at[half, piece, piece],
            )

    def finish(half):
        for piece in range(2):
            for part in (1 - piece, piece):
                sends.landed(cut(landing, (half, piece), part), land_recv.at[half, piece, part])

    return finish


def ring_sum_direct(sends, axis_of, sums, landing, land_recv, ready):
    for step in (2, 1, 3):
        for half in range(2):
            ready(half, step)
            sends.go(
                sends.place.turned(axis_of(half), step),
                sums.at[half, step],
                landing.at[half, step - 1],
                land_recv.at[half, step - 1],
            )
    for half in range(2):
        ready(half, 0)

    def finish(half):
        for step in range(1, SIDE):
            sends.landed(landing.at[half, step - 1], land_recv.at[half, step - 1])

    return finish


def scatter_kernel(
    parts_ref, rows_ref, out_ref, mine, twin, sums, via_one, land_one, halves, land_two,
    both, other,
    local_sem, send_sem, twin_recv, via_one_recv, land_one_recv, land_two_recv,
    far_recv,
):
    place = Place()
    half_rows = parts_ref.shape[4] // 2

    def source(half, group, core):
        rows = pl.ds(half * half_rows, half_rows)
        if half == 0:
            return parts_ref.at[group, :, core, :, rows]
        return parts_ref.at[:, group, core, :, rows]

    barrier = greet(ring_targets(place) + [place.at(dy=1)])
    loads = {}
    order = (2, 1, 3, 0)
    for step in order:
        for half in range(2):
            loads[half, step] = pltpu.make_async_copy(
                source(half, place.along(half, step), place.core),
                mine.at[half, step],
                local_sem.at[half, step],
            )
            loads[half, step].start()
    pl.semaphore_wait(*barrier)
    sends = Sends(place, send_sem)
    for step in order:
        for half in range(2):
            sends.go(
                place.at(dcore=1),
                source(half, place.along(half, step), 1 - place.core),
                twin.at[half, step],
                twin_recv.at[half, step],
            )

    def ready_one(half, step):
        loads[half, step].wait()
        sends.landed(twin.at[half, step], twin_recv.at[half, step])
        sums[half, step] = (wide(mine[half, step]) + wide(twin[half, step])).astype(sums.dtype)

    done_one = ring_sum(
        sends, lambda half: half, sums, via_one, land_one, via_one_recv, land_one_recv, ready_one
    )
    arrived = set()

    def ready_two(half, step):
        if half not in arrived:
            arrived.add(half)
            done_one(half)
        spot = place.along(1 - half, step)
        total = wide(sums[half, 0, spot])
        for side in range(2):
            total = total + wide(land_one[half, side, spot])
        halves[half, step] = total.astype(halves.dtype)

    done_two = ring_sum_direct(
        sends, lambda half: 1 - half, halves, land_two, land_two_recv, ready_two
    )
    for half in range(2):
        done_two(half)
        total = wide(halves[half, 0])
        for side in range(SIDE - 1):
            total = total + wide(land_two[half, side])
        total = total.astype(both.dtype)
        parts = [rows_ref[half * half_rows : (half + 1) * half_rows]]
        parts += [total[head, :, :HEAD] for head in range(GROUP)]
        parts += [total[head, :, HEAD:] for head in range(GROUP)]
        both[half] = jnp.concatenate(parts, axis=1)
    sends.go(place.at(dy=1), both.at[1 - place.y], other, far_recv)
    width = GROUP * HEAD
    kept = both[place.y]
    sends.landed(other, far_recv)
    received = other[...]
    low = jnp.where(place.y == 0, kept, received)
    high = jnp.where(place.y == 0, received, kept)
    parts = []
    for n in range(3):
        parts += [low[:, n * width : (n + 1) * width], high[:, n * width : (n + 1) * width]]
    out_ref[...] = jnp.concatenate(parts, axis=1)
    sends.finish()


def scatter_plane(parts, rows_grad):
    heads, rows, lanes = parts.shape[1:]
    piece = (heads, rows // 2, lanes)
    small = (heads, rows // 4, lanes)
    kind = parts.dtype
    sem = pltpu.SemaphoreType.DMA
    return pl.pallas_call(
        scatter_kernel,
        out_shape=jax.ShapeDtypeStruct((rows // 2, 6 * rows_grad.shape[1]), kind),
        in_specs=[ANYWHERE, VMEM],
        out_specs=pl.BlockSpec(memory_space=pltpu.VMEM),
        scratch_shapes=[
            pltpu.VMEM((2, SIDE, SIDE) + piece, kind),
            pltpu.VMEM((2, SIDE, SIDE) + piece, kind),
            pltpu.VMEM((2, SIDE, SIDE) + piece, kind),
            pltpu.VMEM((2, 2, SIDE) + small, kind),
            pltpu.VMEM((2, 2, SIDE) + piece, kind),
            pltpu.VMEM((2, SIDE) + piece, kind),
            pltpu.VMEM((2, SIDE - 1) + piece, kind),
            pltpu.VMEM((2, rows // 2, 3 * rows_grad.shape[1]), kind),
            pltpu.VMEM((rows // 2, 3 * rows_grad.shape[1]), kind),
            sem((2, SIDE)), sem((33,)), sem((2, SIDE)),
            sem((2, 2)), sem((2, 2, 2)), sem((2, SIDE - 1)), sem,
        ],
        compiler_params=pltpu.CompilerParams(
            collective_id=2, has_side_effects=True, vmem_limit_bytes=60 * 1024 * 1024
        ),
        name="scatter_plane",
    )(parts.reshape((SIDE, SIDE, 2) + parts.shape[1:]), rows_grad)


LANES = 128
UNIT = 16
UNITS = 9
BLOCK_ROWS = UNIT * (UNITS + 1)


def runs(slab_rows):
    found, unit = [], 0
    for slab, rows in enumerate(slab_rows):
        row = 0
        while row < rows:
            block, inside = divmod(unit, UNITS)
            take = min(UNITS - inside, (rows - row) // UNIT)
            found.append((slab, row, block, inside * UNIT, take * UNIT))
            row += take * UNIT
            unit += take
    return found


def block_at(block):
    return block // 32, block // 16 % 2, block // 4 % 4, block % 4


def weights_kernel(
    normed_ref, grads_ref, context_ref, attended_ref, router_ref, slab_ref, ffn_ref, w_query_ref,
    w_key_ref, w_value_ref, tokens_ref, hidden_ref, gain_ref,
    full, input_ref,
    share, share_other, parts, twin, sums, via_one, land_one, halves, land_two, other,
    send_sem, twin_recv, via_one_recv, land_one_recv, land_two_recv,
    far_recv, far_back_recv, two_back_recv, one_back_recv, twin_back_recv, share_recv,
):
    place = Place()
    width = context_ref.shape[1]
    barrier = greet(ring_targets(place) + [place.at(dy=1)], True)
    sends = Sends(place, send_sem)
    partial = jnp.zeros(share.shape, jnp.float32)
    for n, ref in enumerate((w_query_ref, w_key_ref, w_value_ref)):
        partial = partial + contract(grads_ref[:, n * width : (n + 1) * width], ref[...], 1, 1)
    share[...] = partial.astype(share.dtype)
    pl.semaphore_wait(*barrier)
    sends.across(share, share_other, share_recv)
    slabs, table = slab_table(normed_ref.shape[1], width)
    operands = ((normed_ref, grads_ref), (context_ref, attended_ref))
    for index, (output, lane) in enumerate(slabs):
        left, right = operands[output // 3]
        lane = lane if output == 3 else output * width + lane
        grad = contract(left[...], right[:, lane : lane + LANES], 0, 0).astype(parts.dtype)
        for slab, row, block, inside, rows in table:
            if slab == index:
                parts[block_at(block) + (slice(inside, inside + rows),)] = grad[row : row + rows]
    sends.landed(share_other, share_recv)
    grad_normed = wide(share[...]) + wide(share_other[...])
    floats_in = wide(tokens_ref[...])
    scale = lax.rsqrt(jnp.mean(floats_in * floats_in, axis=1, keepdims=True) + EPSILON)
    scaled = gain_ref[...][None] * grad_normed
    input_ref[...] = (
        hidden_ref[...]
        + scale * scaled
        - floats_in * scale**3 * jnp.mean(scaled * floats_in, axis=1, keepdims=True)
    )
    gain_sum = jnp.sum(grad_normed * floats_in * scale, axis=0, keepdims=True)
    tall = router_ref.shape[0] // 2
    router = jnp.concatenate([router_ref[:tall], router_ref[tall:]], axis=1)
    lines = [
        line[:, n : n + LANES]
        for line in (gain_sum, ffn_ref[...])
        for n in range(0, gain_sum.shape[1], LANES)
    ]
    lines.append(jnp.zeros((UNIT - len(lines), LANES), jnp.float32))
    small = [router[n : n + UNIT] for n in range(0, tall, UNIT)]
    small += [slab_ref[n : n + UNIT] for n in range(0, slab_ref.shape[0], UNIT)]
    small.append(jnp.concatenate(lines, axis=0))
    for block in range(64):
        part = small[block] if block < len(small) else jnp.zeros((UNIT, LANES), jnp.float32)
        parts[block_at(block) + (slice(UNIT * UNITS, BLOCK_ROWS),)] = part.astype(parts.dtype)

    order = (2, 1, 3, 0)
    for step in order:
        for half in range(2):
            sends.go(
                place.at(dcore=1),
                parts.at[half, 1 - place.core, place.along(half, step)],
                twin.at[half, step],
                twin_recv.at[half, step],
            )

    def ready_one(half, step):
        sends.landed(twin.at[half, step], twin_recv.at[half, step])
        own = parts[half, place.core, place.along(half, step)]
        sums[half, step] = (wide(own) + wide(twin[half, step])).astype(sums.dtype)

    done_one = ring_sum(
        sends, lambda half: half, sums, via_one, land_one, via_one_recv, land_one_recv, ready_one
    )
    arrived = set()

    def ready_two(half, step):
        if half not in arrived:
            arrived.add(half)
            done_one(half)
        spot = place.along(1 - half, step)
        total = wide(sums[half, 0, spot])
        for side in range(2):
            total = total + wide(land_one[half, side, spot])
        halves[half, step] = total.astype(halves.dtype)

    done_two = ring_sum_direct(
        sends, lambda half: 1 - half, halves, land_two, land_two_recv, ready_two
    )
    low = BLOCK_ROWS // 2
    for half in range(2):
        done_two(half)
        total = wide(halves[half, 0])
        for side in range(SIDE - 1):
            total = total + wide(land_two[half, side])
        halves[half, 0] = total.astype(halves.dtype)
        sends.go(
            place.at(dy=1),
            halves.at[half, 0, pl.ds(pl.multiple_of((1 - place.y) * low, UNIT), low)],
            other.at[half],
            far_recv.at[half],
        )

    def spot(half, core, first, second, rows=None):
        place_of = (half, core, place.along(half, first), place.along(1 - half, second))
        return full.at[place_of] if rows is None else full.at[place_of + (rows,)]

    def y_rows(y):
        return pl.ds(pl.multiple_of(y * low, UNIT), low)

    for half in range(2):
        sends.landed(other.at[half], far_recv.at[half])
        total = wide(halves[half, 0, y_rows(place.y)]) + wide(other[half])
        full[
            half, place.core, place.along(half, 0), place.along(1 - half, 0), y_rows(place.y)
        ] = total.astype(full.dtype)
        view = spot(half, place.core, 0, 0, y_rows(place.y))
        sends.go(place.at(dy=1), view, view, far_back_recv.at[half])

    subs = [pl.ds(piece * low, low) for piece in range(2)]
    for half in range(2):
        sends.landed(
            spot(half, place.core, 0, 0, y_rows(1 - place.y)), far_back_recv.at[half]
        )
        view = spot(half, place.core, 0, 0)
        for step in range(1, SIDE):
            sends.go(
                place.turned(1 - half, step), view, view, two_back_recv.at[half, SIDE - step]
            )

    def group(half, core, first, rows=None):
        if rows is None:
            return full.at[half, core, place.along(half, first)]
        return full.at[half, core, place.along(half, first), :, rows]

    for half in range(2):
        for step in range(1, SIDE):
            sends.landed(spot(half, place.core, 0, step), two_back_recv.at[half, step])
        view = group(half, place.core, 0)
        for step in (1, SIDE - 1):
            sends.go(place.turned(half, step), view, view, one_back_recv.at[half, SIDE - step, 0])
        sends.go(place.at(dcore=1), view, view, twin_back_recv.at[half, 0])
    for half in range(2):
        for piece, step in ((0, 1), (1, SIDE - 1)):
            view = group(half, place.core, SIDE - step)
            sends.landed(view, one_back_recv.at[half, SIDE - step, 0])
            part = group(half, place.core, SIDE - step, subs[piece])
            sends.go(place.turned(half, step), part, part, one_back_recv.at[half, 2, piece])
            sends.go(place.at(dcore=1), view, view, twin_back_recv.at[half, SIDE - step])
    for half in range(2):
        for piece in range(2):
            sends.landed(group(half, place.core, 2, subs[piece]), one_back_recv.at[half, 2, piece])
        view = group(half, place.core, 2)
        sends.go(place.at(dcore=1), view, view, twin_back_recv.at[half, 2])
    for first in (0, 3, 1, 2):
        for half in range(2):
            sends.landed(group(half, 1 - place.core, first), twin_back_recv.at[half, first])

    sends.finish()


def slab_table(tall, width):
    slabs = [(output, lane) for output in range(3) for lane in range(0, width, LANES)]
    slabs += [(3, lane) for lane in range(0, tall, LANES)]
    return slabs, runs([tall if output < 3 else width for output, _ in slabs])


def unpack_kernel(
    full, input_ref, mixed_ref,
    query_ref, key_ref, value_ref, proj_ref, router_ref, slab_ref, gains_ref, grad_input_ref,
    mixed_out_ref,
):
    grad_input_ref[...] = input_ref[...]
    mixed_out_ref[...] = mixed_ref[...]
    slabs, table = slab_table(query_ref.shape[0], query_ref.shape[1])
    for slab, row, block, inside, rows in table:
        output, lane = slabs[slab]
        ref = (query_ref, key_ref, value_ref, proj_ref)[output]
        ref[row : row + rows, lane : lane + LANES] = wide(
            full[block_at(block) + (slice(inside, inside + rows),)]
        )
    tall = router_ref.shape[0] // 2
    experts = router_ref.shape[1]

    def small(block):
        return wide(full[block_at(block) + (slice(UNIT * UNITS, BLOCK_ROWS),)])

    for block in range(tall // UNIT):
        part = small(block)
        for side in range(2):
            start = side * tall + block * UNIT
            router_ref[start : start + UNIT] = part[:, side * experts : (side + 1) * experts]
    base = tall // UNIT
    for block in range(slab_ref.shape[0] // UNIT):
        slab_ref[block * UNIT : (block + 1) * UNIT] = small(base + block)[:, : slab_ref.shape[1]]
    gains_ref[...] = small(base + slab_ref.shape[0] // UNIT)


def weight_totals(
    normed, grads, context, attended, grad_router, slab, grad_ffn, weights, tokens, grad_hidden,
    gain, mixed,
):
    kind = jnp.bfloat16
    tall = normed.shape[1]
    local = context.shape[1]
    piece = (BLOCK_ROWS, LANES)
    part = (BLOCK_ROWS // 2, LANES)
    sem = pltpu.SemaphoreType.DMA
    floats = functools.partial(jax.ShapeDtypeStruct, dtype=jnp.float32)
    full, grad_input = pl.pallas_call(
        weights_kernel,
        out_shape=(
            jax.ShapeDtypeStruct((2, 2, SIDE, SIDE) + piece, kind),
            floats(tokens.shape),
        ),
        in_specs=[VMEM] * 13,
        out_specs=(VMEM,) * 2,
        scratch_shapes=[
            pltpu.VMEM(tokens.shape, kind),
            pltpu.VMEM(tokens.shape, kind),
            pltpu.VMEM((2, 2, SIDE, SIDE) + piece, kind),
            pltpu.VMEM((2, SIDE, SIDE) + piece, kind),
            pltpu.VMEM((2, SIDE, SIDE) + piece, kind),
            pltpu.VMEM((2, 2, SIDE) + part, kind),
            pltpu.VMEM((2, 2, SIDE) + piece, kind),
            pltpu.VMEM((2, SIDE) + piece, kind),
            pltpu.VMEM((2, SIDE - 1) + piece, kind),
            pltpu.VMEM((2,) + part, kind),
            sem((64,)), sem((2, SIDE)),
            sem((2, 2)), sem((2, 2, 2)), sem((2, SIDE - 1)),
            sem((2,)), sem((2,)), sem((2, SIDE)), sem((2, SIDE, 2)), sem((2, SIDE)), sem,
        ],
        compiler_params=pltpu.CompilerParams(
            collective_id=3, has_side_effects=True, vmem_limit_bytes=60 * 1024 * 1024
        ),
        name="weight_totals",
    )(
        normed, grads, context, attended, grad_router, slab, grad_ffn, *weights, tokens,
        grad_hidden, gain,
    )
    return pl.pallas_call(
        unpack_kernel,
        out_shape=(
            floats((tall, local)),
            floats((tall, local)),
            floats((tall, local)),
            floats((local, tall)),
            floats(grad_router.shape),
            floats((slab.shape[0], local // HEAD)),
            floats((UNIT, LANES)),
            floats(tokens.shape),
            jax.ShapeDtypeStruct(tokens.shape, kind),
        ),
        in_specs=[VMEM] * 3,
        out_specs=(VMEM,) * 9,
        compiler_params=pltpu.CompilerParams(vmem_limit_bytes=60 * 1024 * 1024),
        name="unpack",
    )(full, grad_input, mixed)


QUARTERS = 4


def gelu_pair(values):
    root = 0.7978845608028654
    cubic = 0.044715
    square = values * values
    bend = jnp.tanh(root * values * (1.0 + cubic * square))
    active = 0.5 * values * (1.0 + bend)
    slope = 0.5 * (1.0 + bend) + 0.5 * values * (1.0 - bend * bend) * root * (
        1.0 + 3.0 * cubic * square
    )
    return active, slope


def middle_kernel(
    both_ref, tokens_ref, cotangent_ref, proj_ref, gain_ref, router_ref, route_ref, slot_ref,
    w_in_hbm, w_out_hbm,
    mixed_ref, hidden_ref, attended_ref, context_ref, grad_both_ref, grad_router_ref,
    grad_gain_ref, rows_in_ref, rows_grad_ref, activ_ref, grad_pre_ref,
    w_in, w_out, swapped, share, share_other, order, order_t, gather_t, send_one, recv_one,
    send_two, recv_two, sums, sums_other, given,
    load_sem, send_sem, one_send, one_recv, two_send, two_recv, swap_recv, share_recv,
    sums_recv, back_recv,
):
    place = Place()
    me = place.me
    count = 2 * 2 * SIDE * SIDE
    loads = [
        pltpu.make_async_copy(w_in_hbm, w_in, load_sem.at[0]),
        pltpu.make_async_copy(w_out_hbm, w_out, load_sem.at[1]),
    ]
    for load in loads:
        load.start()
    barrier = pltpu.get_barrier_semaphore()

    @pl.loop(1, count)
    def _(step):
        pl.semaphore_signal(
            barrier,
            inc=1,
            device_id={"ctx": lax.rem(me + step, count)},
            device_id_type=pl.DeviceIdType.MESH,
        )

    pl.semaphore_signal(
        barrier,
        inc=1,
        device_id={"mp": 1 - lax.axis_index("mp")},
        device_id_type=pl.DeviceIdType.MESH,
    )
    pl.semaphore_wait(barrier, count)
    sends = Sends(place, send_sem)
    tok_rows = tokens_ref.shape[0]
    first = place.y == 0

    mine = pl.ds(pl.multiple_of(place.y * tok_rows, tok_rows), tok_rows)
    theirs = pl.ds(pl.multiple_of((1 - place.y) * tok_rows, tok_rows), tok_rows)
    sends.go(place.at(dy=1), both_ref.at[theirs], swapped, swap_recv)
    kept = both_ref[mine]
    sends.landed(swapped, swap_recv)
    received = swapped[...]
    context = jnp.concatenate(
        [jnp.where(first, kept, received), jnp.where(first, received, kept)], axis=1
    )
    context_ref[...] = context
    share[...] = contract(context, proj_ref[...], 1, 0).astype(share.dtype)
    sends.across(share, share_other, share_recv)
    spots = tok_rows * QUARTERS
    cells = 16 * count
    route = route_ref[...].astype(jnp.float32)
    spot = route * 16.0 + slot_ref[...].astype(jnp.float32)
    square = (tok_rows, tok_rows)
    diagonal = lax.broadcasted_iota(jnp.int32, square, 0) == lax.broadcasted_iota(
        jnp.int32, square, 1
    )

    def column(line):
        return jnp.sum(jnp.where(diagonal, line, 0.0), axis=1, keepdims=True).astype(jnp.int32)

    spot_row = jnp.concatenate(
        [spot.astype(jnp.int32) + 4 * n for n in range(QUARTERS)], axis=1
    )
    spot_col = column(spot)
    gather = jnp.where(
        lax.broadcasted_iota(jnp.int32, (cells, spots), 0) == spot_row, 1.0, 0.0
    ).astype(jnp.bfloat16)
    sends.landed(share_other, share_recv)
    hidden = wide(tokens_ref[...]) + (wide(share[...]) + wide(share_other[...]))
    scale = lax.rsqrt(jnp.mean(hidden * hidden, axis=1, keepdims=True) + EPSILON)
    normed = hidden * scale * gain_ref[...][None]
    logits = lax.dot_general(
        normed, router_ref[...], (((1,), (0,)), ((), ())), precision=PRECISE,
        preferred_element_type=jnp.float32,
    )
    shifted = jnp.exp(logits - jnp.max(logits, axis=1, keepdims=True))
    probs = shifted / jnp.sum(shifted, axis=1, keepdims=True)
    chosen = jnp.where(
        column(route) == lax.broadcasted_iota(jnp.int32, probs.shape, 1), 1.0, 0.0
    )
    gate = jnp.sum(probs * chosen, axis=1, keepdims=True)
    grad_y = wide(cotangent_ref[...])
    width = 2 * tokens_ref.shape[1] // QUARTERS
    payload = [normed[:, :width], normed[:, width:]]
    payload += [gate * grad_y[:, :width], gate * grad_y[:, width:]]
    payload = jnp.concatenate(payload, axis=0).astype(jnp.bfloat16)
    send_one[...] = (
        contract(gather, payload, 1, 0).astype(send_one.dtype).reshape(send_one.shape)
    )

    def exchange(src, dst, send, recv):
        @pl.loop(1, count)
        def _(step):
            target = lax.rem(me + step, count)
            sender(target, src.at[target], dst.at[me], send.at[step], recv.at[step]).start()

        dst[me] = src[me]

    def arrive(dst, recv):
        @pl.loop(1, count)
        def _(step):
            source = lax.rem(me + count - step, count)
            sends.landed(dst.at[source], recv.at[step])

    exchange(send_one, recv_one, one_send, one_recv)
    rows = cells // QUARTERS

    def cell_of(index):
        row = index & (rows - 1)
        return (row >> 2) * 16 + (index >> 8) * 4 + (row & 3)

    down = lax.broadcasted_iota(jnp.int32, (cells, cells), 0)
    right = lax.broadcasted_iota(jnp.int32, (cells, cells), 1)
    order[...] = jnp.where(cell_of(down) == right, 1.0, 0.0).astype(order.dtype)
    order_t[...] = jnp.where(down == cell_of(right), 1.0, 0.0).astype(order_t.dtype)
    cell = lax.broadcasted_iota(jnp.int32, (tok_rows, cells), 1)
    for n in range(QUARTERS):
        gather_t[n * tok_rows : (n + 1) * tok_rows] = jnp.where(
            spot_col + 4 * n == cell, 1.0, 0.0
        ).astype(gather_t.dtype)
    for load in loads:
        load.wait()
    arrive(recv_one, one_recv)

    got = contract(order[...], recv_one[...].reshape(cells, width), 1, 0).astype(jnp.bfloat16)
    rows_in_ref[...] = jnp.concatenate([got[:rows], got[rows : 2 * rows]], axis=1)
    rows_grad_ref[...] = jnp.concatenate([got[2 * rows : 3 * rows], got[3 * rows :]], axis=1)
    hidden_units = w_in.shape[1]
    chunk = hidden_units // 3
    out = jnp.zeros(rows_in_ref.shape, jnp.float32)
    back = jnp.zeros(rows_in_ref.shape, jnp.float32)
    for start in range(0, hidden_units, chunk):
        units = slice(start, start + chunk)
        active, slope = gelu_pair(contract(rows_in_ref[...], w_in[:, units], 1, 0))
        active = active.astype(jnp.bfloat16)
        activ_ref[:, units] = active
        out = out + contract(active, w_out[units], 1, 0)
        grad_pre = (contract(rows_grad_ref[...], w_out[units], 1, 1) * slope).astype(jnp.bfloat16)
        grad_pre_ref[:, units] = grad_pre
        back = back + contract(grad_pre, w_in[:, units], 1, 1)
    whole = [out[:, :width], out[:, width:], back[:, :width], back[:, width:]]
    whole = jnp.concatenate(whole, axis=0).astype(jnp.bfloat16)
    send_two[...] = (
        contract(order_t[...], whole, 1, 0).astype(send_two.dtype).reshape(send_two.shape)
    )
    exchange(send_two, recv_two, two_send, two_recv)
    arrive(recv_two, two_recv)
    sums[...] = contract(gather_t[...], recv_two[...].reshape(cells, width), 1, 0).astype(
        sums.dtype
    )
    sends.across(sums, sums_other, sums_recv)
    sends.landed(sums_other, sums_recv)
    total = wide(sums[...]) + wide(sums_other[...])
    parts = [total[n * tok_rows : (n + 1) * tok_rows] for n in range(QUARTERS)]
    expert_rows = jnp.concatenate(parts[:2], axis=1).astype(jnp.bfloat16).astype(jnp.float32)
    grad_sent = jnp.concatenate(parts[2:], axis=1).astype(jnp.bfloat16).astype(jnp.float32)

    mixed_ref[...] = (hidden + gate * expert_rows).astype(mixed_ref.dtype)
    grad_gate = jnp.sum(grad_y * expert_rows, axis=1, keepdims=True)
    grad_logits = grad_gate * gate * (chosen - probs)
    grad_router_ref[...] = lax.dot_general(
        normed, grad_logits, (((0,), (0,)), ((), ())), precision=PRECISE,
        preferred_element_type=jnp.float32,
    )
    grad_normed = grad_sent + lax.dot_general(
        grad_logits, router_ref[...], (((1,), (1,)), ((), ())), precision=PRECISE,
        preferred_element_type=jnp.float32,
    )
    scaled = gain_ref[...][None] * grad_normed
    grad_gain_ref[...] = jnp.sum(grad_normed * hidden * scale, axis=0, keepdims=True)
    grad_hidden = (
        grad_y
        + scale * scaled
        - hidden * scale**3 * jnp.mean(scaled * hidden, axis=1, keepdims=True)
    )
    hidden_ref[...] = grad_hidden
    attended = grad_hidden.astype(jnp.bfloat16)
    attended_ref[...] = attended
    grad_context = contract(attended, proj_ref[...], 1, 1).astype(jnp.bfloat16)
    half = grad_context.shape[1] // 2
    left, right_part = grad_context[:, :half], grad_context[:, half:]
    given[...] = jnp.where(first, right_part, left)
    grad_both_ref[mine] = jnp.where(first, left, right_part)
    sends.go(place.at(dy=1), given, grad_both_ref.at[mine], back_recv)
    sends.landed(grad_both_ref.at[theirs], back_recv)
    sends.finish()

    @pl.loop(1, count)
    def _(step):
        for src, send in ((send_one, one_send), (send_two, two_send)):
            sender(me, src.at[0], src.at[0], send.at[step], send.at[step]).wait_send()


def middle(
    both, tokens, cotangent, w_proj, gain, router, w_in, w_out, route, slot
):
    kind = jnp.bfloat16
    tok_rows, wide_row = tokens.shape
    count = router.shape[1]
    rows = 4 * count
    hidden = w_in.shape[1]
    width = 2 * wide_row // QUARTERS
    spots = QUARTERS * tok_rows
    shape = jax.ShapeDtypeStruct
    sem = pltpu.SemaphoreType.DMA
    buffer = pltpu.VMEM((count, 16, width), kind)
    return pl.pallas_call(
        middle_kernel,
        out_shape=(
            shape(tokens.shape, kind),
            shape(tokens.shape, jnp.float32),
            shape(tokens.shape, kind),
            shape((tok_rows, 2 * both.shape[1]), kind),
            shape(both.shape, kind),
            shape(router.shape, jnp.float32),
            shape((1, wide_row), jnp.float32),
            shape((rows, wide_row), kind),
            shape((rows, wide_row), kind),
            shape((rows, hidden), kind),
            shape((rows, hidden), kind),
        ),
        in_specs=[VMEM] * 8 + [ANYWHERE] * 2,
        out_specs=(VMEM,) * 11,
        scratch_shapes=[
            pltpu.VMEM(w_in.shape, kind),
            pltpu.VMEM(w_out.shape, kind),
            pltpu.VMEM((tok_rows, both.shape[1]), kind),
            pltpu.VMEM(tokens.shape, kind),
            pltpu.VMEM(tokens.shape, kind),
            pltpu.VMEM((16 * count, 16 * count), kind),
            pltpu.VMEM((16 * count, 16 * count), kind),
            pltpu.VMEM((spots, 16 * count), kind),
            buffer, buffer, buffer, buffer,
            pltpu.VMEM((spots, width), kind),
            pltpu.VMEM((spots, width), kind),
            pltpu.VMEM((tok_rows, both.shape[1]), kind),
            sem((2,)), sem((4,)), sem((count,)), sem((count,)), sem((count,)), sem((count,)),
            sem, sem, sem, sem,
        ],
        compiler_params=pltpu.CompilerParams(
            collective_id=4, has_side_effects=True, vmem_limit_bytes=60 * 1024 * 1024
        ),
        name="middle",
    )(
        both, tokens, cotangent, w_proj, gain, router, route[None], slot[None], w_in, w_out,
    )


def shards(
    tokens,
    attn_gain,
    w_query,
    w_key,
    w_value,
    w_proj,
    rel_table,
    rel_bucket,
    ffn_gain,
    router,
    w_in,
    w_out,
    expert_route,
    expert_slot,
    cotangent,
):
    me = lax.axis_index("ctx")
    side = 2 * SIDE * SIDE
    place = jnp.stack([me % side, me // side]).astype(jnp.int32)
    normed, rows, held = gather_plane(tokens, attn_gain, w_query, w_key, w_value)

    buckets = jnp.pad(rel_bucket, (0, 1), mode="edge").reshape(BLOCK, BLOCK)
    both, turned, lse, flipped, table, uneven = attend(place, rel_table, buckets, held, rows)
    (
        mixed, grad_hidden1, grad_attended, context, grad_both, grad_router, grad_ffn_gain,
        rows_in, rows_grad, activ, grad_pre,
    ) = middle(
        both, tokens, cotangent, w_proj, ffn_gain, router, w_in[0], w_out[0], expert_route,
        expert_slot,
    )
    grad_parts, grad_rows, slab, grad_expert_in, grad_expert_out = attend_back(
        place, uneven, table, held, rows, grad_both, turned, lse, flipped, rows_in, rows_grad,
        activ, grad_pre, rel_table.shape[0],
    )
    grads = scatter_plane(grad_parts, grad_rows)
    (
        grad_query, grad_key, grad_value, grad_proj, grad_router, grad_table, gains, grad_input,
        mixed,
    ) = weight_totals(
        normed, grads, context, grad_attended, grad_router, slab, grad_ffn_gain,
        (w_query, w_key, w_value), tokens, grad_hidden1, attn_gain, mixed,
    )
    lines = tokens.shape[1] // LANES
    return (
        mixed,
        grad_input,
        gains[:lines].reshape(-1),
        grad_query,
        grad_key,
        grad_value,
        grad_proj,
        grad_table,
        gains[lines : 2 * lines].reshape(-1),
        grad_router,
        grad_expert_in[None],
        grad_expert_out[None],
    )


def solution(mesh):
    return jax.shard_map(
        shards,
        mesh=mesh,
        in_specs=(
            P("ctx", None),
            P(),
            P(None, "mp"),
            P(None, "mp"),
            P(None, "mp"),
            P("mp", None),
            P(None, "mp"),
            P(),
            P(),
            P(),
            P("ctx", None, "mp"),
            P("ctx", "mp", None),
            P("ctx"),
            P("ctx"),
            P("ctx", None),
        ),
        out_specs=(
            P("ctx", None),
            P("ctx", None),
            P(),
            P(None, "mp"),
            P(None, "mp"),
            P(None, "mp"),
            P("mp", None),
            P(None, "mp"),
            P(),
            P(),
            P("ctx", None, "mp"),
            P("ctx", "mp", None),
        ),
        check_vma=False,
    )
```

profile of v0, /device:TPU:1, one launch (start us, length us, event | category | flops | bytes accessed | tf_op | source)
XLA Modules:
  0.0 252.3 jit_solution(6491823993365904959)
XLA Ops:
  0.7 0.6 pad_add_fusion.place_ref
  1.2 1.3 slice.10
  2.5 1.4 copy.27.rel_ref
  3.9 2.2 add_bitcast_fusion.buckets_ref
  6.1 1.8 copy.28.router_ref
  7.9 40.2 %gather_plane.1 = (bf16[128,768]{1,0:T(8,128)(2,1)}, bf16[256,192]{1,0:T(8,128)(2,1)}, bf16[32,3,256,128]{3,2,1,0:T(8,128)(2,1)}) custom-call(bf16[128,768]{1,0:T(8,128)(2,1)} %tokens_ref.5, f32[768]{0:T(1024)} %gain_ref.5, bf16[768,384]{1,0:T(8,128)(2,1)} %w_query_ref.3, bf16[768,384]{1,0:T(8,128)(2,1)} %w_key_ref.3, bf16[768,384]{1,0:T(8,128)(2,1)} %w_value_ref.3), custom_call_target="tpu_custom_call" | custom-call | tf_op jit(solution)/shard_map/gather_plane/pallas_call | solution.py:679
  48.1 14.3 %attend.1 = (bf16[256,192]{1,0:T(8,128)(2,1)}, f32[3,64,256]{2,1,0:T(8,128)}, f32[3,1,256]{2,1,0:T(1,128)}, s32[128,128]{1,0:T(8,128)}, f32[3,128,128]{2,1,0:T(8,128)}, /*index=5*/s32[1,128]{1,0:T(1,128)}) custom-call(s32[2]{0:T(128)} %pad_add_fusion.place_ref, f32[32,6]{1,0:T(8,128)} %copy.27.rel_ref, s32[128,128]{1,0:T(8,128)} %add_bitcast_fusion.buckets_ref, ...), custom_call_target="tpu_custom_call" | custom-call | tf_op jit(solution)/shard_map/attend/pallas_call | solution.py:377
  62.4 69.6 %middle.1 = (bf16[128,768]{1,0:T(8,128)(2,1)}, f32[128,768]{1,0:T(8,128)}, bf16[128,768]{1,0:T(8,128)(2,1)}, bf16[128,384]{1,0:T(8,128)(2,1)}, bf16[256,192]{1,0...) custom-call(bf16[256,192]{1,0:T(8,128)(2,1)} %get-tuple-element.53.b, ...), custom_call_target="tpu_custom_call" | custom-call | tf_op jit(solution)/shard_map/middle/pallas_call | solution.py:1390
  132.0 27.2 %attend_back.1 = (bf16[32,3,256,128]{3,2,1,0:T(8,128)(2,1)}, bf16[256,192]{1,0:T(8,128)(2,1)}, f32[32,128]{1,0:T(8,128)}, f32[768,1536]{1,0:T(8,128)}, f32[1536,768]{1,0:T(8,128)}) custom-call(s32[2]{0:T(128)} %pad_add_fusion.place_ref, s32[1,128]{1,0:T(1,128)} %get-tuple-element.51.uneven_ref, f32[3,128,128]{2,1,0:T(8,128)} %get-tuple-element.52.table_ref, ...), custom_call_target="tpu_custom_call" | custom-call | tf_op jit(solution)/shard_map/attend_back/pallas_call | solution.py:412
  159.2 35.0 %scatter_plane.1.grads_ref = bf16[128,1152]{1,0:T(8,128)(2,1)} custom-call(bf16[4,4,2,3,256,128]{5,4,3,2,1,0:T(8,128)(2,1)} %bitcast.15, bf16[256,192]{1,0:T(8,128)(2,1)} %get-tuple-element.63.rows_ref), custom_call_target="tpu_custom_call" | custom-call | tf_op jit(solution)/shard_map/scatter_plane/pallas_call | solution.py:859
  194.2 48.8 %weight_totals.1 = (bf16[2,2,4,4,160,128]{5,4,3,2,1,0:T(8,128)(2,1)}, f32[128,768]{1,0:T(8,128)}) custom-call(bf16[128,768]{1,0:T(8,128)(2,1)} %get-tuple-element.48.normed_ref, bf16[128,1152]{1,0:T(8,128)(2,1)} %scatter_plane.1.grads_ref, bf16[128,384]{1,0:T(8,128)(2,1)} %get-tuple-element.64.context_ref, bf16[128,768]{1,0:T(8,128)(2,1)} %get-tuple-element.65.attended_ref, ...), custom_call_target="tpu_custom_call" | custom-call | tf_op jit(solution)/shard_map/weight_totals/pallas_call | solution.py:1113
  243.0 4.5 %unpack.1 = (f32[768,384]{1,0:T(8,128)}, f32[768,384]{1,0:T(8,128)}, f32[768,384]{1,0:T(8,128)}, f32[384,768]{1,0:T(8,128)}, f32[768,64]{1,0:T(8,128)}, /*index=...) custom-call(bf16[2,2,4,4,160,128]{5,4,3,2,1,0:T(8,128)(2,1)} %get-tuple-element.70.full, ...), custom_call_target="tpu_custom_call" | custom-call | tf_op jit(solution)/shard_map/unpack/pallas_call | solution.py:1144
  247.5 1.4 copy.29
  248.8 1.4 slice_bitcast_fusion
  250.2 1.8 copy.30
where the time goes:
time: 256 us; the launch traced here: 252 us
  Pallas kernels  239 us (93%)
  local copies, waits for them, and re-layouts  9.04 us (4%)
  other arithmetic  2.77 us (1%)
    pallas_call x1, Pallas kernels, middle(): pl.pallas_call(middle_kernel, out_shape=(shape(tokens.shape, kind), shape...  69.6 us
    pallas_call x1, Pallas kernels, weight_totals(): pl.pallas_call(weights_kernel, out_shape=(jax.ShapeDtypeStruct((2, 2, SID...  48.8 us
    pallas_call x1, Pallas kernels, gather_plane(): pl.pallas_call(gather_kernel, out_shape=(shape(tokens.shape, kind), shape...  40.2 us
    pallas_call x1, Pallas kernels, scatter_plane(): pl.pallas_call(scatter_kernel, out_shape=jax.ShapeDtypeStruct((rows // 2,...  35 us
    pallas_call x1, Pallas kernels, attend_back(): pl.pallas_call(backward_kernel, out_shape=(shape(keys.shape, jnp.bfloat16...  27.2 us
    pallas_call x1, Pallas kernels, attend(): pl.pallas_call(forward_kernel, out_shape=(shape(rows.shape, jnp.bfloat16)...  14.3 us
    unnamed x4, local copies, waits for them, and re-layouts  6.42 us

commit v1 on v0

--- a/solution.py
+++ b/solution.py
@@ -151,8 +151,8 @@
     flags.start()
     for head in range(GROUP):
         values = jnp.zeros((BLOCK, BLOCK), jnp.float32)
-        for bucket in range(rel_ref.shape[0]):
-            value = rel_ref[bucket, place_ref[1] * GROUP + head]
+        for bucket in range(rel_ref.shape[1]):
+            value = rel_ref[place_ref[1] * GROUP + head, bucket]
             values = jnp.where(flipped == bucket, value, values)
         table_ref[head] = values
     fill_turned(query_ref, rows_ref, True)
@@ -768,7 +768,7 @@
 
 def scatter_kernel(
     parts_ref, rows_ref, out_ref, mine, twin, sums, via_one, land_one, halves, land_two,
-    both, other,
+    both, other, rows_other,
     local_sem, send_sem, twin_recv, via_one_recv, land_one_recv, land_two_recv,
     far_recv,
 ):
@@ -794,6 +794,8 @@
             loads[half, step].start()
     pl.semaphore_wait(*barrier)
     sends = Sends(place, send_sem)
+    their_rows = pl.ds(pl.multiple_of((1 - place.y) * half_rows, half_rows), half_rows)
+    sends.go(place.at(dy=1), rows_ref.at[their_rows], rows_other, far_recv.at[1])
     for step in order:
         for half in range(2):
             sends.go(
@@ -832,15 +834,16 @@
         for side in range(SIDE - 1):
             total = total + wide(land_two[half, side])
         total = total.astype(both.dtype)
-        parts = [rows_ref[half * half_rows : (half + 1) * half_rows]]
-        parts += [total[head, :, :HEAD] for head in range(GROUP)]
+        parts = [total[head, :, :HEAD] for head in range(GROUP)]
         parts += [total[head, :, HEAD:] for head in range(GROUP)]
         both[half] = jnp.concatenate(parts, axis=1)
-    sends.go(place.at(dy=1), both.at[1 - place.y], other, far_recv)
+    sends.go(place.at(dy=1), both.at[1 - place.y], other, far_recv.at[0])
     width = GROUP * HEAD
-    kept = both[place.y]
-    sends.landed(other, far_recv)
-    received = other[...]
+    mine_rows = pl.ds(pl.multiple_of(place.y * half_rows, half_rows), half_rows)
+    kept = jnp.concatenate([rows_ref[mine_rows], both[place.y]], axis=1)
+    sends.landed(rows_other, far_recv.at[1])
+    sends.landed(other, far_recv.at[0])
+    received = jnp.concatenate([rows_other[...], other[...]], axis=1)
     low = jnp.where(place.y == 0, kept, received)
     high = jnp.where(place.y == 0, received, kept)
     parts = []
@@ -869,10 +872,11 @@
             pltpu.VMEM((2, 2, SIDE) + piece, kind),
             pltpu.VMEM((2, SIDE) + piece, kind),
             pltpu.VMEM((2, SIDE - 1) + piece, kind),
-            pltpu.VMEM((2, rows // 2, 3 * rows_grad.shape[1]), kind),
-            pltpu.VMEM((rows // 2, 3 * rows_grad.shape[1]), kind),
-            sem((2, SIDE)), sem((33,)), sem((2, SIDE)),
-            sem((2, 2)), sem((2, 2, 2)), sem((2, SIDE - 1)), sem,
+            pltpu.VMEM((2, rows // 2, 2 * rows_grad.shape[1]), kind),
+            pltpu.VMEM((rows // 2, 2 * rows_grad.shape[1]), kind),
+            pltpu.VMEM((rows // 2, rows_grad.shape[1]), kind),
+            sem((2, SIDE)), sem((34,)), sem((2, SIDE)),
+            sem((2, 2)), sem((2, 2, 2)), sem((2, SIDE - 1)), sem((2,)),
         ],
         compiler_params=pltpu.CompilerParams(
             collective_id=2, has_side_effects=True, vmem_limit_bytes=60 * 1024 * 1024
@@ -1082,21 +1086,20 @@
         ref[row : row + rows, lane : lane + LANES] = wide(
             full[block_at(block) + (slice(inside, inside + rows),)]
         )
-    tall = router_ref.shape[0] // 2
-    experts = router_ref.shape[1]
+    experts = router_ref.shape[0]
+    tall = router_ref.shape[1] // 2
 
     def small(block):
         return wide(full[block_at(block) + (slice(UNIT * UNITS, BLOCK_ROWS),)])
 
-    for block in range(tall // UNIT):
-        part = small(block)
-        for side in range(2):
-            start = side * tall + block * UNIT
-            router_ref[start : start + UNIT] = part[:, side * experts : (side + 1) * experts]
     base = tall // UNIT
-    for block in range(slab_ref.shape[0] // UNIT):
-        slab_ref[block * UNIT : (block + 1) * UNIT] = small(base + block)[:, : slab_ref.shape[1]]
-    gains_ref[...] = small(base + slab_ref.shape[0] // UNIT)
+    turned = jnp.concatenate([small(block) for block in range(base)], axis=0).T
+    router_ref[:, :tall] = turned[:experts]
+    router_ref[:, tall:] = turned[experts:]
+    heads, buckets = slab_ref.shape
+    slab = [small(base + block) for block in range(buckets // UNIT)]
+    slab_ref[...] = jnp.concatenate(slab, axis=0).T[:heads]
+    gains_ref[...] = small(base + buckets // UNIT)
 
 
 def weight_totals(
@@ -1148,8 +1151,8 @@
             floats((tall, local)),
             floats((tall, local)),
             floats((local, tall)),
-            floats(grad_router.shape),
-            floats((slab.shape[0], local // HEAD)),
+            floats(grad_router.shape[::-1]),
+            floats((local // HEAD, slab.shape[0])),
             floats((UNIT, LANES)),
             floats(tokens.shape),
             jax.ShapeDtypeStruct(tokens.shape, kind),
@@ -1162,6 +1165,7 @@
 
 
 QUARTERS = 4
+STRIDE = 11
 
 
 def gelu_pair(values):
@@ -1253,7 +1257,7 @@
     scale = lax.rsqrt(jnp.mean(hidden * hidden, axis=1, keepdims=True) + EPSILON)
     normed = hidden * scale * gain_ref[...][None]
     logits = lax.dot_general(
-        normed, router_ref[...], (((1,), (0,)), ((), ())), precision=PRECISE,
+        normed, router_ref[...], (((1,), (1,)), ((), ())), precision=PRECISE,
         preferred_element_type=jnp.float32,
     )
     shifted = jnp.exp(logits - jnp.max(logits, axis=1, keepdims=True))
@@ -1274,16 +1278,14 @@
     def exchange(src, dst, send, recv):
         @pl.loop(1, count)
         def _(step):
-            target = lax.rem(me + step, count)
-            sender(target, src.at[target], dst.at[me], send.at[step], recv.at[step]).start()
+            target = lax.rem(me + step * STRIDE, count)
+            sender(target, src.at[target], dst.at[me], send, recv).start()
 
         dst[me] = src[me]
 
     def arrive(dst, recv):
-        @pl.loop(1, count)
-        def _(step):
-            source = lax.rem(me + count - step, count)
-            sends.landed(dst.at[source], recv.at[step])
+        others = dst.at[pl.ds(0, count - 1)]
+        sends.landed(others, recv)
 
     exchange(send_one, recv_one, one_send, one_recv)
     rows = cells // QUARTERS
@@ -1346,7 +1348,7 @@
         preferred_element_type=jnp.float32,
     )
     grad_normed = grad_sent + lax.dot_general(
-        grad_logits, router_ref[...], (((1,), (1,)), ((), ())), precision=PRECISE,
+        grad_logits, router_ref[...], (((1,), (0,)), ((), ())), precision=PRECISE,
         preferred_element_type=jnp.float32,
     )
     scaled = gain_ref[...][None] * grad_normed
@@ -1368,10 +1370,9 @@
     sends.landed(grad_both_ref.at[theirs], back_recv)
     sends.finish()
 
-    @pl.loop(1, count)
-    def _(step):
-        for src, send in ((send_one, one_send), (send_two, two_send)):
-            sender(me, src.at[0], src.at[0], send.at[step], send.at[step]).wait_send()
+    for src, send in ((send_one, one_send), (send_two, two_send)):
+        others = src.at[pl.ds(0, count - 1)]
+        sender(me, others, others, send, send).wait_send()
 
 
 def middle(
@@ -1379,7 +1380,7 @@
 ):
     kind = jnp.bfloat16
     tok_rows, wide_row = tokens.shape
-    count = router.shape[1]
+    count = router.shape[0]
     rows = 4 * count
     hidden = w_in.shape[1]
     width = 2 * wide_row // QUARTERS
@@ -1395,7 +1396,7 @@
             shape(tokens.shape, kind),
             shape((tok_rows, 2 * both.shape[1]), kind),
             shape(both.shape, kind),
-            shape(router.shape, jnp.float32),
+            shape(router.shape[::-1], jnp.float32),
             shape((1, wide_row), jnp.float32),
             shape((rows, wide_row), kind),
             shape((rows, wide_row), kind),
@@ -1417,8 +1418,7 @@
             pltpu.VMEM((spots, width), kind),
             pltpu.VMEM((spots, width), kind),
             pltpu.VMEM((tok_rows, both.shape[1]), kind),
-            sem((2,)), sem((4,)), sem((count,)), sem((count,)), sem((count,)), sem((count,)),
-            sem, sem, sem, sem,
+            sem((2,)), sem((4,)), sem, sem, sem, sem, sem, sem, sem, sem,
         ],
         compiler_params=pltpu.CompilerParams(
             collective_id=4, has_side_effects=True, vmem_limit_bytes=60 * 1024 * 1024
@@ -1451,13 +1451,13 @@
     place = jnp.stack([me % side, me // side]).astype(jnp.int32)
     normed, rows, held = gather_plane(tokens, attn_gain, w_query, w_key, w_value)
 
-    buckets = jnp.pad(rel_bucket, (0, 1), mode="edge").reshape(BLOCK, BLOCK)
-    both, turned, lse, flipped, table, uneven = attend(place, rel_table, buckets, held, rows)
+    buckets = jnp.pad(rel_bucket, (0, 1), constant_values=31).reshape(BLOCK, BLOCK)
+    both, turned, lse, flipped, table, uneven = attend(place, rel_table.T, buckets, held, rows)
     (
         mixed, grad_hidden1, grad_attended, context, grad_both, grad_router, grad_ffn_gain,
         rows_in, rows_grad, activ, grad_pre,
     ) = middle(
-        both, tokens, cotangent, w_proj, ffn_gain, router, w_in[0], w_out[0], expert_route,
+        both, tokens, cotangent, w_proj, ffn_gain, router.T, w_in[0], w_out[0], expert_route,
         expert_slot,
     )
     grad_parts, grad_rows, slab, grad_expert_in, grad_expert_out = attend_back(
@@ -1481,9 +1481,9 @@
         grad_key,
         grad_value,
         grad_proj,
-        grad_table,
+        grad_table.T,
         gains[lines : 2 * lines].reshape(-1),
-        grad_router,
+        grad_router.T,
         grad_expert_in[None],
         grad_expert_out[None],
     )

time: 256 us -> 242 us (0.945)
  local copies, waits for them, and re-layouts: 9.04 us -> 2.82 us
  Pallas kernels: 239 us -> 235 us
    unnamed x4 -> x0, local copies, waits for them, and re-layouts: 6.42 us -> none
    pallas_call x1, Pallas kernels: 69.6 us -> 64.1 us  [middle(): pl.pallas_call(middle_kernel, out_shape=(shape(tokens.shape, kind), shape...]
where the time goes in v1:
time: 242 us; the launch traced here: 239 us
  Pallas kernels  235 us (97%)
  local copies, waits for them, and re-layouts  2.82 us (1%)
    pallas_call x1, Pallas kernels, middle(): pl.pallas_call(middle_kernel, out_shape=(shape(tokens.shape, kind), shape...  64.1 us
    pallas_call x1, Pallas kernels, weight_totals(): pl.pallas_call(weights_kernel, out_shape=(jax.ShapeDtypeStruct((2, 2, SID...  48.1 us
    pallas_call x1, Pallas kernels, gather_plane(): pl.pallas_call(gather_kernel, out_shape=(shape(tokens.shape, kind), shape...  40.2 us
    pallas_call x1, Pallas kernels, scatter_plane(): pl.pallas_call(scatter_kernel, out_shape=jax.ShapeDtypeStruct((rows // 2,...  36.4 us
    pallas_call x1, Pallas kernels, attend_back(): pl.pallas_call(backward_kernel, out_shape=(shape(keys.shape, jnp.bfloat16...  27.2 us
    pallas_call x1, Pallas kernels, attend(): pl.pallas_call(forward_kernel, out_shape=(shape(rows.shape, jnp.bfloat16)...  14.3 us

profile of v1, /device:TPU:1, one launch (start us, length us, event | category | flops | bytes accessed | tf_op | source)
XLA Modules:
  0.0 239.2 jit_solution(513304174414293256)
XLA Ops:
  0.7 0.6 pad_add_fusion.place_ref
  1.3 1.5 pad_bitcast_fusion.buckets_ref
  2.7 40.2 %gather_plane.1 = (bf16[128,768]{1,0:T(8,128)(2,1)}, bf16[256,192]{1,0:T(8,128)(2,1)}, bf16[32,3,256,128]{3,2,1,0:T(8,128)(2,1)}) custom-call(bf16[128,768]{1,0:T(8,128)(2,1)} %tokens_ref.5, f32[768]{0:T(1024)} %gain_ref.5, bf16[768,384]{1,0:T(8,128)(2,1)} %w_query_ref.3, bf16[768,384]{1,0:T(8,128)(2,1)} %w_key_ref.3, bf16[768,384]{1,0:T(8,128)(2,1)} %w_value_ref.3), custom_call_target="tpu_custom_call" | custom-call | tf_op jit(solution)/shard_map/gather_plane/pallas_call | solution.py:679
  43.0 14.3 %attend.1 = (bf16[256,192]{1,0:T(8,128)(2,1)}, f32[3,64,256]{2,1,0:T(8,128)}, f32[3,1,256]{2,1,0:T(1,128)}, s32[128,128]{1,0:T(8,128)}, f32[3,128,128]{2,1,0:T(8,128)}, /*index=5*/s32[1,128]{1,0:T(1,128)}) custom-call(s32[2]{0:T(128)} %pad_add_fusion.place_ref, f32[6,32]{1,0:T(8,128)} %bitcast.23, s32[128,128]{1,0:T(8,128)} %pad_bitcast_fusion.buckets_ref, ...), custom_call_target="tpu_custom_call" | custom-call | tf_op jit(solution)/shard_map/attend/pallas_call | solution.py:377
  57.3 64.1 %middle.1 = (bf16[128,768]{1,0:T(8,128)(2,1)}, f32[128,768]{1,0:T(8,128)}, bf16[128,768]{1,0:T(8,128)(2,1)}, bf16[128,384]{1,0:T(8,128)(2,1)}, bf16[256,192]{1,0...) custom-call(bf16[256,192]{1,0:T(8,128)(2,1)} %get-tuple-element.53.b, ...), custom_call_target="tpu_custom_call" | custom-call | tf_op jit(solution)/shard_map/middle/pallas_call | solution.py:1391
  121.4 27.2 %attend_back.1 = (bf16[32,3,256,128]{3,2,1,0:T(8,128)(2,1)}, bf16[256,192]{1,0:T(8,128)(2,1)}, f32[32,128]{1,0:T(8,128)}, f32[768,1536]{1,0:T(8,128)}, f32[1536,768]{1,0:T(8,128)}) custom-call(s32[2]{0:T(128)} %pad_add_fusion.place_ref, s32[1,128]{1,0:T(1,128)} %get-tuple-element.51.uneven_ref, f32[3,128,128]{2,1,0:T(8,128)} %get-tuple-element.52.table_ref, ...), custom_call_target="tpu_custom_call" | custom-call | tf_op jit(solution)/shard_map/attend_back/pallas_call | solution.py:412
  148.6 36.4 %scatter_plane.1.grads_ref = bf16[128,1152]{1,0:T(8,128)(2,1)} custom-call(bf16[4,4,2,3,256,128]{5,4,3,2,1,0:T(8,128)(2,1)} %bitcast.19, bf16[256,192]{1,0:T(8,128)(2,1)} %get-tuple-element.63.rows_ref), custom_call_target="tpu_custom_call" | custom-call | tf_op jit(solution)/shard_map/scatter_plane/pallas_call | solution.py:862
  185.0 48.1 %weight_totals.1 = (bf16[2,2,4,4,160,128]{5,4,3,2,1,0:T(8,128)(2,1)}, f32[128,768]{1,0:T(8,128)}) custom-call(bf16[128,768]{1,0:T(8,128)(2,1)} %get-tuple-element.48.normed_ref, bf16[128,1152]{1,0:T(8,128)(2,1)} %scatter_plane.1.grads_ref, bf16[128,384]{1,0:T(8,128)(2,1)} %get-tuple-element.64.context_ref, bf16[128,768]{1,0:T(8,128)(2,1)} %get-tuple-element.65.attended_ref, ...), custom_call_target="tpu_custom_call" | custom-call | tf_op jit(solution)/shard_map/weight_totals/pallas_call | solution.py:1116
  233.1 4.4 %unpack.1 = (f32[768,384]{1,0:T(8,128)}, f32[768,384]{1,0:T(8,128)}, f32[768,384]{1,0:T(8,128)}, f32[384,768]{1,0:T(8,128)}, f32[64,768]{1,0:T(8,128)}, /*index=...) custom-call(bf16[2,2,4,4,160,128]{5,4,3,2,1,0:T(8,128)(2,1)} %get-tuple-element.70.full, ...), custom_call_target="tpu_custom_call" | custom-call | tf_op jit(solution)/shard_map/unpack/pallas_call | solution.py:1147
  237.5 1.3 slice_bitcast_fusion

commit v2 on v1

--- a/solution.py
+++ b/solution.py
@@ -611,13 +611,12 @@
             ring_recv.at[half, slot[0], slot[1], piece or 0],
         )
 
-    def to_twin(half, first, second):
-        sends.go(
-            place.at(dcore=1),
-            held(half, first, second),
-            view(half, first, second, place.core),
-            twin_recv.at[half, first, second],
-        )
+    def whole(dx, dz, core):
+        return out_ref.at[(place.along(0, dx) * SIDE + place.along(1, dz)) * 2 + core]
+
+    def to_twin(dx, dz):
+        src = block_ref if dx == 0 and dz == 0 else whole(dx, dz, place.core)
+        sends.go(place.at(dcore=1), src, whole(dx, dz, place.core), twin_recv.at[dx, dz])
 
     def wait(half, first, second):
         if second == 2:
@@ -644,13 +643,14 @@
         for stage in range(2):
             for step in (1, -1, 2)[: 3 - stage]:
                 shift(half, 0, 0, stage, step)
-        to_twin(half, 0, 0)
+    to_twin(0, 0)
     own = pltpu.make_async_copy(
         block_ref, out_ref.at[(place.x * SIDE + place.z) * 2 + place.core], local_sem
     )
     own.start()
     order = [(3, 0), (1, 0), (0, 3), (0, 1), (2, 0), (3, 3), (3, 1), (1, 3), (1, 1), (0, 2)]
     order += [(3, 2), (1, 2), (2, 3), (2, 1), (2, 2)]
+    passed = set()
     for first, second in order:
         for half in range(2):
             wait(half, first, second)
@@ -659,12 +659,12 @@
                     shift(half, first, second, 1, step)
             else:
                 relay(half, first, second)
-            to_twin(half, first, second)
-    for first, second in [(0, 0)] + order:
-        for half in range(2):
-            sends.landed(
-                view(half, first, second, 1 - place.core), twin_recv.at[half, first, second]
-            )
+        passed.add((first, second))
+        if (second, first) in passed:
+            for dx, dz in sorted({(first, second), (second, first)}):
+                to_twin(dx, dz)
+    for dx, dz in [(0, 0)] + order:
+        sends.landed(whole(dx, dz, 1 - place.core), twin_recv.at[dx, dz])
     own.wait()
     sends.finish()
 
@@ -689,7 +689,7 @@
             pltpu.VMEM(block, kind),
             pltpu.VMEM((3, tok_rows, width), kind),
             pltpu.VMEM((3, tok_rows, width), kind),
-            sem, sem((73,)), sem((2, SIDE, SIDE, 2)), sem((2, SIDE, SIDE)), sem,
+            sem, sem((73,)), sem((2, SIDE, SIDE, 2)), sem((SIDE, SIDE)), sem,
         ],
         compiler_params=pltpu.CompilerParams(
             collective_id=1, has_side_effects=True, vmem_limit_bytes=60 * 1024 * 1024
@@ -1216,9 +1216,28 @@
         device_id={"mp": 1 - lax.axis_index("mp")},
         device_id_type=pl.DeviceIdType.MESH,
     )
+    tok_rows = tokens_ref.shape[0]
+    spots = tok_rows * QUARTERS
+    cells = 16 * count
+    route = route_ref[...].astype(jnp.float32)
+    spot = route * 16.0 + slot_ref[...].astype(jnp.float32)
+    square = (tok_rows, tok_rows)
+    diagonal = lax.broadcasted_iota(jnp.int32, square, 0) == lax.broadcasted_iota(
+        jnp.int32, square, 1
+    )
+
+    def column(line):
+        return jnp.sum(jnp.where(diagonal, line, 0.0), axis=1, keepdims=True).astype(jnp.int32)
+
+    spot_row = jnp.concatenate(
+        [spot.astype(jnp.int32) + 4 * n for n in range(QUARTERS)], axis=1
+    )
+    spot_col = column(spot)
+    gather = jnp.where(
+        lax.broadcasted_iota(jnp.int32, (cells, spots), 0) == spot_row, 1.0, 0.0
+    ).astype(jnp.bfloat16)
     pl.semaphore_wait(barrier, count)
     sends = Sends(place, send_sem)
-    tok_rows = tokens_ref.shape[0]
     first = place.y == 0
 
     mine = pl.ds(pl.multiple_of(place.y * tok_rows, tok_rows), tok_rows)
@@ -1233,25 +1252,6 @@
     context_ref[...] = context
     share[...] = contract(context, proj_ref[...], 1, 0).astype(share.dtype)
     sends.across(share, share_other, share_recv)
-    spots = tok_rows * QUARTERS
-    cells = 16 * count
-    route = route_ref[...].astype(jnp.float32)
-    spot = route * 16.0 + slot_ref[...].astype(jnp.float32)
-    square = (tok_rows, tok_rows)
-    diagonal = lax.broadcasted_iota(jnp.int32, square, 0) == lax.broadcasted_iota(
-        jnp.int32, square, 1
-    )
-
-    def column(line):
-        return jnp.sum(jnp.where(diagonal, line, 0.0), axis=1, keepdims=True).astype(jnp.int32)
-
-    spot_row = jnp.concatenate(
-        [spot.astype(jnp.int32) + 4 * n for n in range(QUARTERS)], axis=1
-    )
-    spot_col = column(spot)
-    gather = jnp.where(
-        lax.broadcasted_iota(jnp.int32, (cells, spots), 0) == spot_row, 1.0, 0.0
-    ).astype(jnp.bfloat16)
     sends.landed(share_other, share_recv)
     hidden = wide(tokens_ref[...]) + (wide(share[...]) + wide(share_other[...]))
     scale = lax.rsqrt(jnp.mean(hidden * hidden, axis=1, keepdims=True) + EPSILON)

time: 242 us -> 242 us (level)
  no operation moved by 1% of the time
where the time goes in v2:
time: 242 us; the launch traced here: 239 us
  Pallas kernels  235 us (97%)
  local copies, waits for them, and re-layouts  2.82 us (1%)
    pallas_call x1, Pallas kernels, middle(): pl.pallas_call(middle_kernel, out_shape=(shape(tokens.shape, kind), shape...  64.3 us
    pallas_call x1, Pallas kernels, weight_totals(): pl.pallas_call(weights_kernel, out_shape=(jax.ShapeDtypeStruct((2, 2, SID...  48.6 us
    pallas_call x1, Pallas kernels, gather_plane(): pl.pallas_call(gather_kernel, out_shape=(shape(tokens.shape, kind), shape...  40.1 us
    pallas_call x1, Pallas kernels, scatter_plane(): pl.pallas_call(scatter_kernel, out_shape=jax.ShapeDtypeStruct((rows // 2,...  35.6 us
    pallas_call x1, Pallas kernels, attend_back(): pl.pallas_call(backward_kernel, out_shape=(shape(keys.shape, jnp.bfloat16...  27.2 us
    pallas_call x1, Pallas kernels, attend(): pl.pallas_call(forward_kernel, out_shape=(shape(rows.shape, jnp.bfloat16)...  14.3 us

profile of v2, /device:TPU:1, one launch (start us, length us, event | category | flops | bytes accessed | tf_op | source)
XLA Modules:
  0.0 238.9 jit_solution(18354052233786641518)
XLA Ops:
  0.7 0.6 pad_add_fusion.place_ref
  1.3 1.5 pad_bitcast_fusion.buckets_ref
  2.7 40.1 %gather_plane.1 = (bf16[128,768]{1,0:T(8,128)(2,1)}, bf16[256,192]{1,0:T(8,128)(2,1)}, bf16[32,3,256,128]{3,2,1,0:T(8,128)(2,1)}) custom-call(bf16[128,768]{1,0:T(8,128)(2,1)} %tokens_ref.5, f32[768]{0:T(1024)} %gain_ref.5, bf16[768,384]{1,0:T(8,128)(2,1)} %w_query_ref.3, bf16[768,384]{1,0:T(8,128)(2,1)} %w_key_ref.3, bf16[768,384]{1,0:T(8,128)(2,1)} %w_value_ref.3), custom_call_target="tpu_custom_call" | custom-call | tf_op jit(solution)/shard_map/gather_plane/pallas_call | solution.py:679
  42.8 14.3 %attend.1 = (bf16[256,192]{1,0:T(8,128)(2,1)}, f32[3,64,256]{2,1,0:T(8,128)}, f32[3,1,256]{2,1,0:T(1,128)}, s32[128,128]{1,0:T(8,128)}, f32[3,128,128]{2,1,0:T(8,128)}, /*index=5*/s32[1,128]{1,0:T(1,128)}) custom-call(s32[2]{0:T(128)} %pad_add_fusion.place_ref, f32[6,32]{1,0:T(8,128)} %bitcast.23, s32[128,128]{1,0:T(8,128)} %pad_bitcast_fusion.buckets_ref, ...), custom_call_target="tpu_custom_call" | custom-call | tf_op jit(solution)/shard_map/attend/pallas_call | solution.py:377
  57.1 64.3 %middle.1 = (bf16[128,768]{1,0:T(8,128)(2,1)}, f32[128,768]{1,0:T(8,128)}, bf16[128,768]{1,0:T(8,128)(2,1)}, bf16[128,384]{1,0:T(8,128)(2,1)}, bf16[256,192]{1,0...) custom-call(bf16[256,192]{1,0:T(8,128)(2,1)} %get-tuple-element.53.b, ...), custom_call_target="tpu_custom_call" | custom-call | tf_op jit(solution)/shard_map/middle/pallas_call | solution.py:1391
  121.4 27.2 %attend_back.1 = (bf16[32,3,256,128]{3,2,1,0:T(8,128)(2,1)}, bf16[256,192]{1,0:T(8,128)(2,1)}, f32[32,128]{1,0:T(8,128)}, f32[768,1536]{1,0:T(8,128)}, f32[1536,768]{1,0:T(8,128)}) custom-call(s32[2]{0:T(128)} %pad_add_fusion.place_ref, s32[1,128]{1,0:T(1,128)} %get-tuple-element.51.uneven_ref, f32[3,128,128]{2,1,0:T(8,128)} %get-tuple-element.52.table_ref, ...), custom_call_target="tpu_custom_call" | custom-call | tf_op jit(solution)/shard_map/attend_back/pallas_call | solution.py:412
  148.6 35.6 %scatter_plane.1.grads_ref = bf16[128,1152]{1,0:T(8,128)(2,1)} custom-call(bf16[4,4,2,3,256,128]{5,4,3,2,1,0:T(8,128)(2,1)} %bitcast.19, bf16[256,192]{1,0:T(8,128)(2,1)} %get-tuple-element.63.rows_ref), custom_call_target="tpu_custom_call" | custom-call | tf_op jit(solution)/shard_map/scatter_plane/pallas_call | solution.py:862
  184.3 48.6 %weight_totals.1 = (bf16[2,2,4,4,160,128]{5,4,3,2,1,0:T(8,128)(2,1)}, f32[128,768]{1,0:T(8,128)}) custom-call(bf16[128,768]{1,0:T(8,128)(2,1)} %get-tuple-element.48.normed_ref, bf16[128,1152]{1,0:T(8,128)(2,1)} %scatter_plane.1.grads_ref, bf16[128,384]{1,0:T(8,128)(2,1)} %get-tuple-element.64.context_ref, bf16[128,768]{1,0:T(8,128)(2,1)} %get-tuple-element.65.attended_ref, ...), custom_call_target="tpu_custom_call" | custom-call | tf_op jit(solution)/shard_map/weight_totals/pallas_call | solution.py:1116
  232.9 4.4 %unpack.1 = (f32[768,384]{1,0:T(8,128)}, f32[768,384]{1,0:T(8,128)}, f32[768,384]{1,0:T(8,128)}, f32[384,768]{1,0:T(8,128)}, f32[64,768]{1,0:T(8,128)}, /*index=...) custom-call(bf16[2,2,4,4,160,128]{5,4,3,2,1,0:T(8,128)(2,1)} %get-tuple-element.70.full, ...), custom_call_target="tpu_custom_call" | custom-call | tf_op jit(solution)/shard_map/unpack/pallas_call | solution.py:1147
  237.3 1.3 slice_bitcast_fusion

commit v3 on v2

--- a/solution.py
+++ b/solution.py
@@ -1333,12 +1333,17 @@
     sums[...] = contract(gather_t[...], recv_two[...].reshape(cells, width), 1, 0).astype(
         sums.dtype
     )
-    sends.across(sums, sums_other, sums_recv)
-    sends.landed(sums_other, sums_recv)
-    total = wide(sums[...]) + wide(sums_other[...])
-    parts = [total[n * tok_rows : (n + 1) * tok_rows] for n in range(QUARTERS)]
-    expert_rows = jnp.concatenate(parts[:2], axis=1).astype(jnp.bfloat16).astype(jnp.float32)
-    grad_sent = jnp.concatenate(parts[2:], axis=1).astype(jnp.bfloat16).astype(jnp.float32)
+    pairs = [pl.ds(n * 2 * tok_rows, 2 * tok_rows) for n in range(2)]
+    for n, pair in enumerate(pairs):
+        sends.across(sums.at[pair], sums_other.at[pair], sums_recv.at[n])
+
+    def summed(n):
+        sends.landed(sums_other.at[pairs[n]], sums_recv.at[n])
+        total = wide(sums[pairs[n]]) + wide(sums_other[pairs[n]])
+        total = jnp.concatenate([total[:tok_rows], total[tok_rows:]], axis=1)
+        return total.astype(jnp.bfloat16).astype(jnp.float32)
+
+    expert_rows = summed(0)
 
     mixed_ref[...] = (hidden + gate * expert_rows).astype(mixed_ref.dtype)
     grad_gate = jnp.sum(grad_y * expert_rows, axis=1, keepdims=True)
@@ -1347,10 +1352,11 @@
         normed, grad_logits, (((0,), (0,)), ((), ())), precision=PRECISE,
         preferred_element_type=jnp.float32,
     )
-    grad_normed = grad_sent + lax.dot_general(
+    grad_normed = lax.dot_general(
         grad_logits, router_ref[...], (((1,), (0,)), ((), ())), precision=PRECISE,
         preferred_element_type=jnp.float32,
     )
+    grad_normed = summed(1) + grad_normed
     scaled = gain_ref[...][None] * grad_normed
     grad_gain_ref[...] = jnp.sum(grad_normed * hidden * scale, axis=0, keepdims=True)
     grad_hidden = (
@@ -1418,7 +1424,7 @@
             pltpu.VMEM((spots, width), kind),
             pltpu.VMEM((spots, width), kind),
             pltpu.VMEM((tok_rows, both.shape[1]), kind),
-            sem((2,)), sem((4,)), sem, sem, sem, sem, sem, sem, sem, sem,
+            sem((2,)), sem((5,)), sem, sem, sem, sem, sem, sem, sem((2,)), sem,
         ],
         compiler_params=pltpu.CompilerParams(
             collective_id=4, has_side_effects=True, vmem_limit_bytes=60 * 1024 * 1024

time: 242 us -> 241 us (level)
  no operation moved by 1% of the time
where the time goes in v3:
time: 241 us; the launch traced here: 238 us
  Pallas kernels  234 us (97%)
  local copies, waits for them, and re-layouts  2.82 us (1%)
    pallas_call x1, Pallas kernels, middle(): pl.pallas_call(middle_kernel, out_shape=(shape(tokens.shape, kind), shape...  63.5 us
    pallas_call x1, Pallas kernels, weight_totals(): pl.pallas_call(weights_kernel, out_shape=(jax.ShapeDtypeStruct((2, 2, SID...  48.7 us
    pallas_call x1, Pallas kernels, gather_plane(): pl.pallas_call(gather_kernel, out_shape=(shape(tokens.shape, kind), shape...  40.1 us
    pallas_call x1, Pallas kernels, scatter_plane(): pl.pallas_call(scatter_kernel, out_shape=jax.ShapeDtypeStruct((rows // 2,...  35.6 us
    pallas_call x1, Pallas kernels, attend_back(): pl.pallas_call(backward_kernel, out_shape=(shape(keys.shape, jnp.bfloat16...  27.2 us
    pallas_call x1, Pallas kernels, attend(): pl.pallas_call(forward_kernel, out_shape=(shape(rows.shape, jnp.bfloat16)...  14.3 us

profile of v3, /device:TPU:1, one launch (start us, length us, event | category | flops | bytes accessed | tf_op | source)
XLA Modules:
  0.0 238.2 jit_solution(13696168084536519461)
XLA Ops:
  0.7 0.6 pad_add_fusion.place_ref
  1.3 1.5 pad_bitcast_fusion.buckets_ref
  2.7 40.1 %gather_plane.1 = (bf16[128,768]{1,0:T(8,128)(2,1)}, bf16[256,192]{1,0:T(8,128)(2,1)}, bf16[32,3,256,128]{3,2,1,0:T(8,128)(2,1)}) custom-call(bf16[128,768]{1,0:T(8,128)(2,1)} %tokens_ref.5, f32[768]{0:T(1024)} %gain_ref.5, bf16[768,384]{1,0:T(8,128)(2,1)} %w_query_ref.3, bf16[768,384]{1,0:T(8,128)(2,1)} %w_key_ref.3, bf16[768,384]{1,0:T(8,128)(2,1)} %w_value_ref.3), custom_call_target="tpu_custom_call" | custom-call | tf_op jit(solution)/shard_map/gather_plane/pallas_call | solution.py:679
  42.8 14.3 %attend.1 = (bf16[256,192]{1,0:T(8,128)(2,1)}, f32[3,64,256]{2,1,0:T(8,128)}, f32[3,1,256]{2,1,0:T(1,128)}, s32[128,128]{1,0:T(8,128)}, f32[3,128,128]{2,1,0:T(8,128)}, /*index=5*/s32[1,128]{1,0:T(1,128)}) custom-call(s32[2]{0:T(128)} %pad_add_fusion.place_ref, f32[6,32]{1,0:T(8,128)} %bitcast.23, s32[128,128]{1,0:T(8,128)} %pad_bitcast_fusion.buckets_ref, ...), custom_call_target="tpu_custom_call" | custom-call | tf_op jit(solution)/shard_map/attend/pallas_call | solution.py:377
  57.1 63.5 %middle.1 = (bf16[128,768]{1,0:T(8,128)(2,1)}, f32[128,768]{1,0:T(8,128)}, bf16[128,768]{1,0:T(8,128)(2,1)}, bf16[128,384]{1,0:T(8,128)(2,1)}, bf16[256,192]{1,0...) custom-call(bf16[256,192]{1,0:T(8,128)(2,1)} %get-tuple-element.53.b, ...), custom_call_target="tpu_custom_call" | custom-call | tf_op jit(solution)/shard_map/middle/pallas_call | solution.py:1397
  120.6 27.2 %attend_back.1 = (bf16[32,3,256,128]{3,2,1,0:T(8,128)(2,1)}, bf16[256,192]{1,0:T(8,128)(2,1)}, f32[32,128]{1,0:T(8,128)}, f32[768,1536]{1,0:T(8,128)}, f32[1536,768]{1,0:T(8,128)}) custom-call(s32[2]{0:T(128)} %pad_add_fusion.place_ref, s32[1,128]{1,0:T(1,128)} %get-tuple-element.51.uneven_ref, f32[3,128,128]{2,1,0:T(8,128)} %get-tuple-element.52.table_ref, ...), custom_call_target="tpu_custom_call" | custom-call | tf_op jit(solution)/shard_map/attend_back/pallas_call | solution.py:412
  147.8 35.6 %scatter_plane.1.grads_ref = bf16[128,1152]{1,0:T(8,128)(2,1)} custom-call(bf16[4,4,2,3,256,128]{5,4,3,2,1,0:T(8,128)(2,1)} %bitcast.19, bf16[256,192]{1,0:T(8,128)(2,1)} %get-tuple-element.63.rows_ref), custom_call_target="tpu_custom_call" | custom-call | tf_op jit(solution)/shard_map/scatter_plane/pallas_call | solution.py:862
  183.4 48.7 %weight_totals.1 = (bf16[2,2,4,4,160,128]{5,4,3,2,1,0:T(8,128)(2,1)}, f32[128,768]{1,0:T(8,128)}) custom-call(bf16[128,768]{1,0:T(8,128)(2,1)} %get-tuple-element.48.normed_ref, bf16[128,1152]{1,0:T(8,128)(2,1)} %scatter_plane.1.grads_ref, bf16[128,384]{1,0:T(8,128)(2,1)} %get-tuple-element.64.context_ref, bf16[128,768]{1,0:T(8,128)(2,1)} %get-tuple-element.65.attended_ref, ...), custom_call_target="tpu_custom_call" | custom-call | tf_op jit(solution)/shard_map/weight_totals/pallas_call | solution.py:1116
  232.1 4.4 %unpack.1 = (f32[768,384]{1,0:T(8,128)}, f32[768,384]{1,0:T(8,128)}, f32[768,384]{1,0:T(8,128)}, f32[384,768]{1,0:T(8,128)}, f32[64,768]{1,0:T(8,128)}, /*index=...) custom-call(bf16[2,2,4,4,160,128]{5,4,3,2,1,0:T(8,128)(2,1)} %get-tuple-element.70.full, ...), custom_call_target="tpu_custom_call" | custom-call | tf_op jit(solution)/shard_map/unpack/pallas_call | solution.py:1147
  236.5 1.3 slice_bitcast_fusion
